TPU v7x, 128 devices: a whole 4x4x4 slice. The times are simulated.
128 devices in a mesh: latent: 16 (over y, z), dp: 8 (over x, core).
Axes of the slice: x: 4, y: 4, z: 4, core: 2. Of those that a mesh axis runs over, the one named last changes fastest.
Arguments:
- residual: bfloat16 [1024, 4608], P('dp', 'latent'), may hold values from -6 to 6
- encoder: bfloat16 [4608, 131072], P(None, ('latent', 'dp')), may hold values from -0.09375 to 0.09375
- encoder_bias: float32 [131072], P(('latent', 'dp')), may hold values from -3 to 3
- thresholds: int32 [131072], P(('latent', 'dp')), may hold values from 32 to 255
- decoder: bfloat16 [131072, 4608], P(('latent', 'dp')), may hold values from -0.03125 to 0.03125
- decoder_bias: float32 [4608], replicated, may hold values from -4 to 4
- probes: bfloat16 [131072, 64], P(('latent', 'dp')), may hold values from -0.03125 to 0.03125
- probe_bias: float32 [64], replicated, may hold values from -4 to 4
- labels: int32 [1024, 64], replicated, may hold values 0 or 1
Outputs:
- error: float32 [1024], P(('latent', 'dp'))
- probe_grad: float32 [131072, 64], P(('latent', 'dp'))
- bias_grad: float32 [64], replicated
- mean_loss: float32 [], replicated
All inputs are finite; a program needn't handle non-finite values.
Results may differ from a plain program's by a relative error of at most 0.00075.
Values may be sent and summed in bfloat16 or wider, within the bound.
No kernel may reach another device: no remote copies, remote signals or barrier semaphores. Data moves between devices by JAX's collectives and lax.ppermute only.
A program may use at most 192 MiB of HBM per device.

v0:
```python
import functools

import jax
import jax.numpy as jnp
from jax import lax
from jax.experimental import pallas as pl
from jax.experimental.pallas import tpu as pltpu
from jax.sharding import PartitionSpec as P

softness = 0.1
levels = 256.0
AXES = ("latent", "dp")
F32 = jnp.float32
BF16 = jnp.bfloat16
KB = 1152
D = 4608
W = D + 128
WR = W + 256
W2 = D + 512
C = D // 2
W3 = D + 1024
VMEM_LIMIT = 8 * 1024 * 1024
LITTLE = pl.CostEstimate(flops=1000000, bytes_accessed=0, transcendentals=0)


def flat(y, z, x, c):
    return ((y * 4 + z) * 4 + x) * 2 + c


def coords():
    for y in range(4):
        for z in range(4):
            for x in range(4):
                for c in range(2):
                    yield {"y": y, "z": z, "x": x}, c


def place(p, c):
    return flat(p["y"], p["z"], p["x"], c)


def pull_perm(axis0, axis1, step):
    pairs = []
    for p, c in coords():
        axis = (axis0, axis1)[c]
        q = dict(p)
        q[axis] = (p[axis] + step) % 4
        pairs.append((place(q, c), place(p, c)))
    return pairs


def pull(value, axis0, axis1, step):
    return lax.ppermute(value, AXES, pull_perm(axis0, axis1, step))


def swap(value):
    pairs = [(place(p, c), place(p, 1 - c)) for p, c in coords()]
    return lax.ppermute(value, AXES, pairs)


def absolute(parts, start):
    twice = jnp.stack(list(parts) * 2)
    return lax.dynamic_slice_in_dim(twice, lax.rem(4 - start, 4), 4, 0)


def load_kernel(source, target, sems):
    pieces = sems.shape[0]
    rows = source.shape[0] // pieces
    copies = []
    for i in range(pieces):
        span = slice(rows * i, rows * (i + 1))
        copies.append(pltpu.make_async_copy(source.at[span], target.at[span], sems.at[i]))
    for copy in copies:
        copy.start()
    for copy in copies:
        copy.wait()


def load(value):
    held = pl.pallas_call(
        load_kernel,
        in_specs=[pl.BlockSpec(memory_space=pltpu.HBM)],
        out_specs=pl.BlockSpec(memory_space=pltpu.VMEM),
        out_shape=jax.ShapeDtypeStruct(value.shape, value.dtype),
        scratch_shapes=[pltpu.SemaphoreType.DMA((4,))],
        compiler_params=pltpu.CompilerParams(vmem_limit_bytes=VMEM_LIMIT),
        cost_estimate=LITTLE,
        name="load",
    )(pltpu.with_memory_space_constraint(value, pltpu.HBM))
    return near(held)


def near(value):
    return pltpu.with_memory_space_constraint(value, pltpu.VMEM)


STAGES = (0, 1, 3, 2)


def encode_kernel(stage, which, tile, where, *refs):
    count = 1 if which is None else 2
    blocks = refs[: 2 * count if which is None else count]
    refs = refs[len(blocks) :]
    enc, bias, cut = refs[:3]
    acc = None if stage == STAGES[0] else refs[3]
    xa, ya = refs[-2:]
    core, y = where[0], where[2]
    depth = 4 // count

    def rows(step):
        return pl.ds(pl.multiple_of(lax.rem(y + step, 4) * KB, KB), KB)

    def activate(preact, cols):
        cutoff = cut[:, cols].astype(F32) / levels
        gate = jax.nn.sigmoid((preact - cutoff) / softness)
        return (preact * gate).astype(BF16)

    def tiles(work):
        @pl.loop(0, enc.shape[1] // tile)
        def _(n):
            work(pl.ds(pl.multiple_of(n * tile, tile), tile))

    def few(parts):
        def work(cols):
            pre = bias[:, cols] + sum(
                jnp.dot(
                    parts[j // depth][j % depth], enc[rows(j), cols], preferred_element_type=F32
                )
                for j in range(4)
            )
            xa[:, cols] = activate(pre, cols)

        tiles(work)

    def many(parts):
        def work(cols):
            for i in range(count):
                part = jnp.dot(
                    parts[i][...].reshape(128 * depth, KB),
                    enc[rows(stage), cols],
                    preferred_element_type=F32,
                )
                span = slice(128 * depth * i, 128 * depth * (i + 1))
                if acc is not None:
                    part = part + acc[span, cols]
                if stage == STAGES[-1]:
                    ya[span, cols] = activate(part + bias[:, cols], cols)
                else:
                    ya[span, cols] = part

        tiles(work)

    for turn in (0, 1):

        @pl.when(core == turn)
        def _(turn=turn):
            if which is None:
                few([blocks[turn]])
                many([blocks[1 - turn]])
            elif which == turn:
                few(blocks)
            else:
                many(blocks)


def encode(stage, which, where, blocks, enc, bias, cut, acc, done=()):
    lat = enc.shape[1]
    vmem = pl.BlockSpec(memory_space=pltpu.VMEM)
    args = [*blocks, enc, bias, cut]
    aliases = {}
    if acc is not None:
        args.append(acc)
        if stage != STAGES[-1]:
            aliases = {len(args): 1}
    for i, value in enumerate(done):
        args.append(value)
        aliases[len(args)] = i
    return pl.pallas_call(
        functools.partial(encode_kernel, stage, which, 256),
        in_specs=[pl.BlockSpec(memory_space=pltpu.SMEM)] + [vmem] * len(args),
        out_specs=[vmem, vmem],
        out_shape=[
            jax.ShapeDtypeStruct((128, lat), BF16),
            jax.ShapeDtypeStruct((512, lat), BF16 if stage == STAGES[-1] else F32),
        ],
        input_output_aliases=aliases,
        compiler_params=pltpu.CompilerParams(vmem_limit_bytes=VMEM_LIMIT),
        cost_estimate=LITTLE,
        name="encode",
    )(where, *args)


def split(total):
    lane = lax.broadcasted_iota(jnp.int32, total.shape, total.ndim - 1)
    high = total.astype(BF16).astype(F32)
    return jnp.where(lane < 64, high, total - high)


def joined(pair):
    return pair + pltpu.roll(pair, 64, pair.ndim - 1)


def decode_kernel(step, tile, where, xa, ya, dec, probes, keep, send0, send1, lhs):
    core = where[0]
    pick = lax.rem(where[2] + step - where[1] + 4, 4)
    lhs[pl.ds(pl.multiple_of(core * 128, 128), 128), :] = xa[...]
    lhs[pl.ds(pl.multiple_of((1 - core) * 128, 128), 128), :] = ya[pick]
    logits = split(jnp.dot(lhs[...], probes[...], preferred_element_type=F32)).astype(BF16)
    keep[:, D:] = logits[:128]
    send1[:, C:] = logits[128:]

    for n in range(D // tile):
        cols = slice(tile * n, tile * (n + 1))
        send, start = (send0, tile * n) if tile * n < C else (send1, tile * n - C)
        out = jnp.dot(lhs[...], dec[:, cols], preferred_element_type=F32).astype(BF16)
        keep[:, cols] = out[:128]
        send[:, start : start + tile] = out[128:]


def decode(step, where, xa, ya, dec, probes):
    lat = dec.shape[0]
    vmem = pl.BlockSpec(memory_space=pltpu.VMEM)
    return pl.pallas_call(
        functools.partial(decode_kernel, step, 768),
        in_specs=[pl.BlockSpec(memory_space=pltpu.SMEM)] + [vmem] * 4,
        out_specs=[vmem] * 3,
        scratch_shapes=[pltpu.VMEM((256, lat), BF16)],
        out_shape=[jax.ShapeDtypeStruct((128, w), BF16) for w in (W, C, W - C)],
        compiler_params=pltpu.CompilerParams(vmem_limit_bytes=VMEM_LIMIT),
        cost_estimate=LITTLE,
        name="decode",
    )(where, xa, ya, dec, probes)


def small_call(kernel, name, outs, *args, scalars=1, scratch=()):
    vmem = pl.BlockSpec(memory_space=pltpu.VMEM)
    smem = pl.BlockSpec(memory_space=pltpu.SMEM)
    return pl.pallas_call(
        kernel,
        in_specs=[smem] * scalars + [vmem] * (len(args) - scalars),
        out_specs=[vmem] * len(outs),
        out_shape=[jax.ShapeDtypeStruct(shape, kind) for shape, kind in outs],
        scratch_shapes=list(scratch),
        compiler_params=pltpu.CompilerParams(vmem_limit_bytes=VMEM_LIMIT),
        cost_estimate=LITTLE,
        name=name,
    )(*args)


def pair_kernel(shift, a, b0, b1, *refs):
    low, high = slice(0, C), slice(C, D)
    outs = refs if shift is None else refs[1:]
    for i in range(2):
        rows = slice(64 * i, 64 * (i + 1))
        out, spot = (outs[i], slice(0, 64)) if shift is None else (outs[0], rows)
        for cols, other in ((low, b0[rows]), (high, b1[rows, :C])):
            part = a[rows, cols].astype(F32) + other.astype(F32)
            if i == shift:
                part = part + refs[0][:, cols].astype(F32)
            out[spot, cols] = part.astype(BF16)
        logits = a[rows, D:].astype(F32) + b1[rows, C:].astype(F32)
        if i == shift:
            logits = logits + refs[0][:, D:W].astype(F32)
        out[spot, D:W] = split(joined(logits)).astype(BF16)
        if shift is None:
            out[:, W:] = jnp.zeros((64, WR - W), BF16)


def pair_sum(shift, *args):
    outs = [((64, WR), BF16)] * 2 if shift is None else [((128, W), BF16)]
    kernel = functools.partial(pair_kernel, shift)
    return small_call(kernel, "pair_sum", outs, *args, scalars=0)


def first_kernel(where, a0, b0, b1, g1, g3, *outs):
    spot = where[5]
    logits = b1[:, C:].astype(F32) + sum(r[:, D:].astype(F32) for r in (a0, g1, g3))
    logits = split(joined(logits)).astype(BF16)
    for d, out in enumerate(outs):
        rows = pl.ds(pl.multiple_of(lax.rem(spot + d, 4) * 32, 32), 32)
        for cols, other in ((slice(0, C), b0[rows, :]), (slice(C, D), b1[rows, :C])):
            part = other.astype(F32) + sum(r[rows, cols].astype(F32) for r in (a0, g1, g3))
            out[:, cols] = part.astype(BF16)
        for k in range(4):
            out[:, D + 128 * k : D + 128 * (k + 1)] = logits[32 * k : 32 * (k + 1)]


def second_kernel(where, m0, g1, g2, g3, *refs):
    outs, total, wide = refs[:4], refs[4], refs[5]
    spot = where[6]

    def four(cols):
        a0, a1, a2, a3 = (r[:, cols].astype(F32) for r in (m0, g1, g2, g3))
        return (a0 + a2) + (a1 + a3)

    total[...] = four(slice(0, D))
    for k in range(4):
        cols = slice(D + 128 * k, D + 128 * (k + 1))
        l0, l1, l2, l3 = (joined(r[:, cols].astype(F32)) for r in (m0, g1, g2, g3))
        wide[32 * k : 32 * (k + 1), :] = (l0 + l2) + (l1 + l3)
    lane = lax.broadcasted_iota(jnp.int32, (8, 128), 1)
    packed = [
        jnp.where(lane < 64, wide[8 * i : 8 * i + 8, :], wide[64 + 8 * i : 72 + 8 * i, :])
        for i in range(8)
    ]
    for d, out in enumerate(outs):
        rows = pl.ds(pl.multiple_of(lax.rem(spot + d, 4) * 8, 8), 8)
        out[:, :D] = total[rows, :]
        for i in range(8):
            out[:, D + 128 * i : D + 128 * (i + 1)] = packed[i]


def third_kernel(m0, g1, g2, g3, tokens, bias, err, logits):
    def four(cols):
        a0, a1, a2, a3 = (r[:, cols] for r in (m0, g1, g2, g3))
        return (a0 + a2) + (a1 + a3)

    gap = tokens[...] - (four(slice(0, D)) + bias[...])
    err[...] = jnp.broadcast_to(jnp.sum(gap * gap, axis=1, keepdims=True) / D, err.shape)
    logits[...] = four(slice(D, W3))


def collect_kernel(*refs):
    for i, ref in enumerate(refs[:4]):
        refs[4][i] = ref[...]


def collect(parts):
    shape = (4, *parts[0].shape)
    return small_call(collect_kernel, "collect", [(shape, parts[0].dtype)], *parts, scalars=0)[0]


def settle_kernel(source, target):
    target[...] = source[...]


def settle(value):
    outs = [(value.shape, value.dtype)]
    return small_call(settle_kernel, "settle", outs, value, scalars=0)[0]


def halves_kernel(a, b, low, high):
    low[...] = a[:2]
    high[...] = b[2:]


def halves(a, b):
    shape = (2, *a.shape[1:])
    outs = [(shape, a.dtype)] * 2
    return small_call(halves_kernel, "halves", outs, a, b, scalars=0)


def rows_kernel(where, block, side1, low, high, side3, out, wide):
    core, x, y = where[0], where[1], where[2]
    start = where[5] * 32 + where[6] * 8
    even = pl.ds(pl.multiple_of(start // 16 * 16, 16), 16)
    turn = lax.rem(y - x + 4, 4)

    def put(j, value):
        wide[...] = value.astype(F32)
        rows = pl.ds(pl.multiple_of(lax.rem(start, 16), 8), 8)
        out[:, pl.ds(pl.multiple_of(lax.rem(y + j, 4) * KB, 128), KB)] = wide[rows, :]

    @pl.when(core == 0)
    def _():
        for j in range(4):
            put(j, block[j, even, :])

    @pl.when(core == 1)
    def _():
        put(0, block[turn, even, :])
        put(1, side1[turn, even, :])
        put(3, side3[turn, even, :])

        @pl.when(turn < 2)
        def _():
            put(2, low[jnp.minimum(turn, 1), even, :])

        @pl.when(turn >= 2)
        def _():
            put(2, high[jnp.maximum(turn - 2, 0), even, :])


def finish_kernel(groups, where, own, oth, labels, bias, *refs):
    actives, ya = refs[:4], refs[4]
    grad, bias_grad, loss, logits, slopes = refs[5:]
    core, x, y = where[0], where[1], where[2]
    lane = lax.broadcasted_iota(jnp.int32, (8, 128), 1)

    def unpack(source, start, parity):
        for d in range(4):
            g = lax.rem(start + d, 4) * 2 + parity
            for i in range(8):
                tile = source[d, :, 128 * i : 128 * (i + 1)]
                logits[g, 8 * i : 8 * i + 8, :] = tile
                logits[g, 64 + 8 * i : 72 + 8 * i, :] = pltpu.roll(tile, 64, 1)

    @pl.when(core == 0)
    def _():
        unpack(own, x, 0)
        unpack(oth, y, 1)

    @pl.when(core == 1)
    def _():
        unpack(oth, x, 0)
        unpack(own, y, 1)

    slopes[...] = jnp.zeros_like(slopes)
    total = jnp.zeros((128, 64), F32)
    sums = jnp.zeros((1, 64), F32)
    for g in range(groups):
        value = logits[g, :, :64] + bias[...]
        target = labels[128 * g : 128 * (g + 1), :].astype(F32)
        slope = (jax.nn.sigmoid(value) - target).astype(BF16)
        slopes[g, :, :64] = slope
        total = total + (jax.nn.softplus(value) - target * value)
        sums = sums + jnp.sum(slope.astype(F32), axis=0, keepdims=True)
    loss[...] = jnp.broadcast_to(
        jnp.sum(jnp.sum(total, axis=1, keepdims=True), axis=0, keepdims=True) / (groups * 128 * 64),
        loss.shape,
    )
    bias_grad[...] = sums / 128

    turned = jnp.zeros((128, ya.shape[2]), F32)
    for d in range(4):
        g = lax.rem(x + d, 4) * 2
        for active, slope in ((actives[d][...], slopes[g]), (ya[d], slopes[g + 1])):
            turned = turned + lax.dot_general(
                slope, active, (((0,), (0,)), ((), ())), preferred_element_type=F32
            )
    grad[...] = (turned / 128)[:64]


def on_device(
    residual, encoder, encoder_bias, thresholds, decoder, decoder_bias, probes, probe_bias, labels
):
    per_group = residual.shape[0]
    lat = encoder.shape[1]
    pos = lax.axis_index(AXES)
    core = pos % 2
    x, z, y = (pos // 2) % 4, (pos // 8) % 4, pos // 32
    is0 = core == 0
    first = jnp.where(is0, x, y)
    second = jnp.where(is0, y, z)
    third = jnp.where(is0, z, x)
    where = jnp.stack([core, x, y, z, first, second, third]).astype(jnp.int32)
    probes2 = jnp.concatenate([probes, probes], axis=1)

    parts = [residual] + [pull(residual, "z", "z", d) for d in (1, 2, 3)]
    unit = absolute(parts, z).transpose(1, 0, 2).reshape(per_group, KB)
    unit, where, probes2, encoder, decoder = lax.optimization_barrier(
        (unit, where, probes2, encoder, decoder)
    )
    unit = settle(unit)
    unit, encoder, decoder = lax.optimization_barrier((unit, encoder, decoder))
    encoder, decoder = load(encoder), load(decoder)
    pulled = [pull(unit, "y", "x", d) for d in (1, 2, 3)]
    unit, pulled, encoder, decoder = lax.optimization_barrier((unit, pulled, encoder, decoder))
    block = collect([unit, *pulled])
    other = swap(block)
    sides = {d: pull(block, "x", "y", d) for d in (1, 3)}

    cut = thresholds[None]
    bias = encoder_bias[None]
    xa = {}

    def run(stage, blocks, acc):
        xa[stage], acc = encode(stage, None, where, blocks, encoder, bias, cut, acc)
        return acc

    acc = run(0, [block, other], None)
    sides, acc = lax.optimization_barrier((sides, acc))
    low, high = halves(sides[1], sides[3])
    far = [pull(low, "x", "y", 1), pull(high, "x", "y", 3)]
    acc = run(1, [sides[1], swap(sides[1])], acc)
    acc = run(3, [sides[3], swap(sides[3])], acc)
    far, acc = lax.optimization_barrier((far, acc))
    mixed = encode(2, 0, where, far, encoder, bias, cut, acc)
    others = [swap(half) for half in far]
    xa[2], acc = encode(2, 1, where, others, encoder, bias, cut, acc, mixed)
    ya = acc.reshape(4, 128, lat)

    keep, got = {}, {}

    def part(d, left):
        keep[d], *send = decode(d, where, left, ya, decoder, probes2)
        got[d] = [swap(half) for half in send]

    part(2, xa[2])
    over = pair_sum(None, keep[2], *got[2])
    over, left1, left3 = lax.optimization_barrier((over, xa[1], xa[3]))
    through = [pull(over[0], "x", "y", 3), pull(over[1], "x", "y", 1)]
    part(1, left1)
    part(3, left3)
    through, keep[1], keep[3], left0 = lax.optimization_barrier(
        (through, keep[1], keep[3], xa[0])
    )
    (message1,) = pair_sum(0, keep[1], *got[1], through[0])
    (message3,) = pair_sum(1, keep[3], *got[3], through[1])
    message1, message3, left0 = lax.optimization_barrier((message1, message3, left0))
    part(0, left0)
    mine = {1: pull(message1, "x", "y", 3), 3: pull(message3, "x", "y", 1)}
    (tokens,) = small_call(
        rows_kernel, "own_rows", [((8, D), F32)],
        where, block, sides[1], *far, sides[3], scratch=[pltpu.VMEM((16, KB), F32)],
    )

    m2 = small_call(
        first_kernel, "first_sum", [((32, W2), BF16)] * 4,
        where, keep[0], *got[0], mine[1], mine[3],
    )
    g2 = [pull(m2[d], "y", "z", 4 - d) for d in (1, 2, 3)]
    m3 = small_call(
        second_kernel, "second_sum", [((8, W3), F32)] * 4, where, m2[0], *g2,
        scratch=[pltpu.VMEM((32, D), F32), pltpu.VMEM((128, 128), F32)],
    )
    g3 = [pull(m3[d], "z", "x", 4 - d) for d in (1, 2, 3)]
    err, packed = small_call(
        third_kernel, "third_sum", [((8, 128), F32), ((8, 1024), F32)],
        m3[0], *g3, tokens, decoder_bias[None], scalars=0,
    )
    owners = []
    for p, c in coords():
        s = (p["x"], p["y"], p["z"]) if c == 0 else (p["y"], p["z"], p["x"])
        owners.append((place(p, c), s[0] * 32 + c * 16 + s[1] * 4 + s[2]))

    pulled = [pull(packed, "x", "y", d) for d in (1, 2, 3)]
    err = lax.ppermute(err, AXES, owners)
    pulled, packed, err = lax.optimization_barrier((pulled, packed, err))
    mine = collect([packed, *pulled])
    theirs = swap(mine)
    error = err[:, 0]
    probe_grad, bias_grad, mean_loss = small_call(
        functools.partial(finish_kernel, 8), "finish",
        [((64, lat), F32), ((1, 64), F32), ((1, 128), F32)],
        where, mine, theirs, labels, probe_bias[None], xa[0], xa[1], xa[2], xa[3], ya,
        scratch=[pltpu.VMEM((8, 128, 128), F32), pltpu.VMEM((8, 128, 128), BF16)],
    )
    return (error, probe_grad.T, bias_grad[0], mean_loss[0, 0])


def solution(mesh):
    in_specs = (
        P("dp", "latent"),
        P(None, ("latent", "dp")),
        P(("latent", "dp")),
        P(("latent", "dp")),
        P(("latent", "dp"), None),
        P(),
        P(("latent", "dp"), None),
        P(),
        P(),
    )
    out_specs = (P(("latent", "dp")), P(("latent", "dp"), None), P(), P())
    return jax.shard_map(
        on_device, mesh=mesh, in_specs=in_specs, out_specs=out_specs, check_vma=False
    )
```

profile of v0, /device:TPU:26, one launch (start us, length us, event | category | flops | bytes accessed | tf_op | source)
XLA Modules:
  0.0 151.4 jit_solution(9826426865671074683)
XLA Ops:
  0.6 4.1 %collective-permute-start = (bf16[128,288]{0,1:T(8,128)(2,1)}, bf16[128,288]{0,1:T(8,128)(2,1)S(1)}, u32[]{:S(2)}, u32[]{:S(2)}) collective-permute-start(bf16[128,288]{0,1:T(8,128)(2,1)} %param.9), channel_id=1, source_target_pairs={{8,0},{9,1},{10,2},{11,3},{12,4},{13,5},{14,6},{15,7},{16,8},{17,9... | collective-permute-start | bytes 221192 | tf_op jit(solution)/shard_map/ppermute | solution.py:53
  8.3 2.7 %collective-permute-done.1 = bf16[128,288]{0,1:T(8,128)(2,1)S(1)} collective-permute-done((bf16[128,288]{0,1:T(8,128)(2,1)}, bf16[128,288]{0,1:T(8,128)(2,1)S(1)}, u32[]{:S(2)}, u32[]{:S(2)}) %collective-permute-start.1) | collective-permute-done | bytes 73760 | tf_op jit(solution)/shard_map/ppermute | solution.py:53
  13.6 2.2 %collective-permute-start.5 = (bf16[128,1152]{1,0:T(8,128)(2,1)S(1)}, bf16[128,1152]{1,0:T(8,128)(2,1)S(1)}, u32[]{:S(2)}, u32[]{:S(2)}) collective-permute-start(bf16[128,1152]{1,0:T(8,128)(2,1)S(1)} %settle.1.refs_0_), channel_id=1, source_target_pairs={{96,0},{7,1},{98,2},{1,3},{100,4},{3,5},{102,6},{5,7},{104,8},{15,... | collective-permute-start | bytes 884744 | tf_op jit(solution)/shard_map/ppermute | solution.py:53
  15.8 3.8 %load.2.refs_2_ = bf16[4608,1024]{1,0:T(8,128)(2,1)S(1)} custom-call(bf16[4608,1024]{1,0:T(8,128)(2,1)} %source), custom_call_target="tpu_custom_call" | custom-call | flops 1000000 | tf_op jit(solution)/shard_map/load/pallas_call | solution.py:80
  19.6 3.8 %load.3.dec = bf16[1024,4608]{1,0:T(8,128)(2,1)S(1)} custom-call(bf16[1024,4608]{1,0:T(8,128)(2,1)} %source.1), custom_call_target="tpu_custom_call" | custom-call | flops 1000000 | tf_op jit(solution)/shard_map/load/pallas_call | solution.py:80
  26.9 4.9 %encode.5 = (bf16[128,1024]{1,0:T(8,128)(2,1)S(1)}, f32[512,1024]{1,0:T(8,128)S(1)}) custom-call(s32[7]{0:T(128)S(1)} %stack.55.where, bf16[4,128,1152]{2,1,0:T(8,128)(2,1)S(1)} %collect.2.refs_0_.block, bf16[4,128,1152]{2,1,0:T(8,128)(2,1)S(1)} %collective-permute-done.8.refs_1_, bf16[4608,1024]{1,0:T(8,128)(2,1)S(1)} %load.2.refs_2_, ...), custom_call_target="tpu_custom_call" | custom-call | flops 1000000 | tf_op jit(solution)/shard_map/encode/pallas_call | solution.py:178
  31.8 8.6 %collective-permute-done.6.a.refs_0_.side1 = bf16[4,128,1152]{2,1,0:T(8,128)(2,1)S(1)} collective-permute-done((bf16[4,128,1152]{2,1,0:T(8,128)(2,1)S(1)}, bf16[4,128,1152]{2,1,0:T(8,128)(2,1)S(1)}, u32[]{:S(2)}, u32[]{:S(2)}) %collective-permute-start.6) | collective-permute-done | bytes 1179680 | tf_op jit(solution)/shard_map/ppermute | solution.py:53
  43.1 2.6 %collective-permute-start.9 = (bf16[2,128,1152]{2,1,0:T(8,128)(2,1)S(1)}, bf16[2,128,1152]{2,1,0:T(8,128)(2,1)S(1)}, u32[]{:S(2)}, u32[]{:S(2)}) collective-permute-start(bf16[2,128,1152]{2,1,0:T(8,128)(2,1)S(1)} %get-tuple-element.95), channel_id=1, source_target_pairs={{2,0},{33,1},{4,2},{35,3},{6,4},{37,5},{0,6},{39,7},{10,8},{41,9},... | collective-permute-start | bytes 1769480 | tf_op jit(solution)/shard_map/ppermute | solution.py:53
  45.6 4.9 %encode.6 = (bf16[128,1024]{1,0:T(8,128)(2,1)S(1)}, f32[512,1024]{1,0:T(8,128)S(1)}) custom-call(s32[7]{0:T(128)S(1)} %stack.55.where, bf16[4,128,1152]{2,1,0:T(8,128)(2,1)S(1)} %collective-permute-done.6.a.refs_0_.side1, bf16[4,128,1152]{2,1,0:T(8,128)(2,1)S(1)} %collective-permute-done.12.refs_1_, ...), custom_call_target="tpu_custom_call", output_to_operand_aliasing={{1}: (6, {})} | custom-call | flops 1000000 | tf_op jit(solution)/shard_map/encode/pallas_call | solution.py:178
  50.5 4.9 %encode.7 = (bf16[128,1024]{1,0:T(8,128)(2,1)S(1)}, f32[512,1024]{1,0:T(8,128)S(1)}) custom-call(s32[7]{0:T(128)S(1)} %stack.55.where, bf16[4,128,1152]{2,1,0:T(8,128)(2,1)S(1)} %collective-permute-done.7.b.refs_0_.side3, bf16[4,128,1152]{2,1,0:T(8,128)(2,1)S(1)} %collective-permute-done.11.refs_1_, ...), custom_call_target="tpu_custom_call", output_to_operand_aliasing={{1}: (6, {})} | custom-call | flops 1000000 | tf_op jit(solution)/shard_map/encode/pallas_call | solution.py:178
  56.0 3.0 %encode.8 = (bf16[128,1024]{1,0:T(8,128)(2,1)S(1)}, bf16[512,1024]{1,0:T(8,128)(2,1)S(1)}) custom-call(s32[7]{0:T(128)S(1)} %stack.55.where, bf16[2,128,1152]{2,1,0:T(8,128)(2,1)S(1)} %collective-permute-done.9.refs_0_.low, bf16[2,128,1152]{2,1,0:T(8,128)(2,1)S(1)} %collective-permute-done.10.refs_1_.high, bf16[4608,1024]{1,0:T(8,128)(2,1)S(1)} %load.2.refs_2_, ...), custom_call_target="tpu_custom_call" | custom-call | flops 1000000 | tf_op jit(solution)/shard_map/encode/pallas_call | solution.py:178
  59.0 2.9 %encode.9 = (bf16[128,1024]{1,0:T(8,128)(2,1)S(1)}, bf16[512,1024]{1,0:T(8,128)(2,1)S(1)}) custom-call(s32[7]{0:T(128)S(1)} %stack.55.where, bf16[2,128,1152]{2,1,0:T(8,128)(2,1)S(1)} %collective-permute-done.13.refs_0_, bf16[2,128,1152]{2,1,0:T(8,128)(2,1)S(1)} %collective-permute-done.14.refs_1_, ...), custom_call_target="tpu_custom_call", output_to_operand_aliasing={{0}: (7, {}), {1}: (8, {})} | custom-call | flops 1000000 | tf_op jit(solution)/shard_map/encode/pallas_call | solution.py:178
  61.9 3.4 %decode.4 = (bf16[128,4736]{1,0:T(8,128)(2,1)S(1)}, bf16[128,2304]{1,0:T(8,128)(2,1)S(1)}, bf16[128,2432]{1,0:T(8,128)(2,1)S(1)}) custom-call(s32[7]{0:T(128)S(1)} %stack.55.where, bf16[128,1024]{1,0:T(8,128)(2,1)S(1)} %get-tuple-element.105.xa.refs_2_, bf16[4,128,1024]{2,1,0:T(8,128)(2,1)S(1)} %bitcast.30, bf16[1024,4608]{1,0:T(8,128)(2,1)S(1)} %load.3.dec, ...), custom_call_target="tpu_custom_call" | custom-call | flops 1000000 | tf_op jit(solution)/shard_map/decode/pallas_call | solution.py:223
  66.0 2.4 %collective-permute-done.15.b0 = bf16[128,2304]{1,0:T(8,128)(2,1)S(1)} collective-permute-done((bf16[128,2304]{1,0:T(8,128)(2,1)S(1)}, bf16[128,2304]{1,0:T(8,128)(2,1)S(1)}, u32[]{:S(2)}, u32[]{:S(2)}) %collective-permute-start.15) | collective-permute-done | bytes 589856 | tf_op jit(solution)/shard_map/ppermute | solution.py:58
  69.5 2.7 %collective-permute-start.18 = (bf16[64,4992]{1,0:T(8,128)(2,1)S(1)}, bf16[64,4992]{1,0:T(8,128)(2,1)S(1)}, u32[]{:S(2)}, u32[]{:S(2)}) collective-permute-start(bf16[64,4992]{1,0:T(8,128)(2,1)S(1)} %get-tuple-element.117), channel_id=1, source_target_pairs={{2,0},{33,1},{4,2},{35,3},{6,4},{37,5},{0,6},{39,7},{10,8},{41,9},... | collective-permute-start | bytes 1916936 | tf_op jit(solution)/shard_map/ppermute | solution.py:53
  72.2 3.4 %decode.6 = (bf16[128,4736]{1,0:T(8,128)(2,1)S(1)}, bf16[128,2304]{1,0:T(8,128)(2,1)S(1)}, bf16[128,2432]{1,0:T(8,128)(2,1)S(1)}) custom-call(s32[7]{0:T(128)S(1)} %stack.55.where, bf16[128,1024]{1,0:T(8,128)(2,1)S(1)} %get-tuple-element.120.xa.refs_3_, bf16[4,128,1024]{2,1,0:T(8,128)(2,1)S(1)} %bitcast.31, bf16[1024,4608]{1,0:T(8,128)(2,1)S(1)} %load.3.dec, ...), custom_call_target="tpu_custom_call" | custom-call | flops 1000000 | tf_op jit(solution)/shard_map/decode/pallas_call | solution.py:223
  75.7 3.4 %decode.5 = (bf16[128,4736]{1,0:T(8,128)(2,1)S(1)}, bf16[128,2304]{1,0:T(8,128)(2,1)S(1)}, bf16[128,2432]{1,0:T(8,128)(2,1)S(1)}) custom-call(s32[7]{0:T(128)S(1)} %stack.55.where, bf16[128,1024]{1,0:T(8,128)(2,1)S(1)} %get-tuple-element.118.xa.refs_1_, bf16[4,128,1024]{2,1,0:T(8,128)(2,1)S(1)} %bitcast.32, bf16[1024,4608]{1,0:T(8,128)(2,1)S(1)} %load.3.dec, ...), custom_call_target="tpu_custom_call" | custom-call | flops 1000000 | tf_op jit(solution)/shard_map/decode/pallas_call | solution.py:223
  84.6 2.5 %collective-permute-start.26 = (bf16[128,4736]{1,0:T(8,128)(2,1)S(1)}, bf16[128,4736]{1,0:T(8,128)(2,1)S(1)}, u32[]{:S(2)}, u32[]{:S(2)}) collective-permute-start(bf16[128,4736]{1,0:T(8,128)(2,1)S(1)} %pair_sum.5), channel_id=1, source_target_pairs={{2,0},{33,1},{4,2},{35,3},{6,4},{37,5},{0,6},{39,7},{10,8},{41,9},... | collective-permute-start | bytes 3637256 | tf_op jit(solution)/shard_map/ppermute | solution.py:53
  87.0 3.4 %decode.7 = (bf16[128,4736]{1,0:T(8,128)(2,1)S(1)}, bf16[128,2304]{1,0:T(8,128)(2,1)S(1)}, bf16[128,2432]{1,0:T(8,128)(2,1)S(1)}) custom-call(s32[7]{0:T(128)S(1)} %stack.55.where, bf16[128,1024]{1,0:T(8,128)(2,1)S(1)} %get-tuple-element.132.xa.refs_0_, bf16[4,128,1024]{2,1,0:T(8,128)(2,1)S(1)} %bitcast.33, bf16[1024,4608]{1,0:T(8,128)(2,1)S(1)} %load.3.dec, ...), custom_call_target="tpu_custom_call" | custom-call | flops 1000000 | tf_op jit(solution)/shard_map/decode/pallas_call | solution.py:223
  91.0 2.4 %collective-permute-done.23.b0 = bf16[128,2304]{1,0:T(8,128)(2,1)S(1)} collective-permute-done((bf16[128,2304]{1,0:T(8,128)(2,1)S(1)}, bf16[128,2304]{1,0:T(8,128)(2,1)S(1)}, u32[]{:S(2)}, u32[]{:S(2)}) %collective-permute-start.23) | collective-permute-done | bytes 589856 | tf_op jit(solution)/shard_map/ppermute | solution.py:58
  93.4 8.1 %collective-permute-done.25.g1 = bf16[128,4736]{1,0:T(8,128)(2,1)S(1)} collective-permute-done((bf16[128,4736]{1,0:T(8,128)(2,1)S(1)}, bf16[128,4736]{1,0:T(8,128)(2,1)S(1)}, u32[]{:S(2)}, u32[]{:S(2)}) %collective-permute-start.25) | collective-permute-done | bytes 1212448 | tf_op jit(solution)/shard_map/ppermute | solution.py:53
  103.8 2.7 %collective-permute-start.27 = (bf16[32,5120]{1,0:T(8,128)(2,1)S(1)}, bf16[32,5120]{1,0:T(8,128)(2,1)S(1)}, u32[]{:S(2)}, u32[]{:S(2)}) collective-permute-start(bf16[32,5120]{1,0:T(8,128)(2,1)S(1)} %get-tuple-element.139), channel_id=1, source_target_pairs={{96,0},{25,1},{98,2},{27,3},{100,4},{29,5},{102,6},{31,7},{104,8},... | collective-permute-start | bytes 983048 | tf_op jit(solution)/shard_map/ppermute | solution.py:53
  107.4 7.2 %collective-permute-done.27.g1 = bf16[32,5120]{1,0:T(8,128)(2,1)S(1)} collective-permute-done((bf16[32,5120]{1,0:T(8,128)(2,1)S(1)}, bf16[32,5120]{1,0:T(8,128)(2,1)S(1)}, u32[]{:S(2)}, u32[]{:S(2)}) %collective-permute-start.27) | collective-permute-done | bytes 327712 | tf_op jit(solution)/shard_map/ppermute | solution.py:53
  115.2 3.1 %collective-permute-done.29.g3 = bf16[32,5120]{1,0:T(8,128)(2,1)S(1)} collective-permute-done((bf16[32,5120]{1,0:T(8,128)(2,1)S(1)}, bf16[32,5120]{1,0:T(8,128)(2,1)S(1)}, u32[]{:S(2)}, u32[]{:S(2)}) %collective-permute-start.29) | collective-permute-done | bytes 327712 | tf_op jit(solution)/shard_map/ppermute | solution.py:53
  119.3 2.3 %collective-permute-start.31 = (f32[8,5632]{1,0:T(8,128)S(1)}, f32[8,5632]{1,0:T(8,128)S(1)}, u32[]{:S(2)}, u32[]{:S(2)}) collective-permute-start(f32[8,5632]{1,0:T(8,128)S(1)} %get-tuple-element.144), channel_id=1, source_target_pairs={{16,0},{5,1},{18,2},{7,3},{20,4},{1,5},{22,6},{3,7},{24,8},{13,9},... | collective-permute-start | bytes 540680 | tf_op jit(solution)/shard_map/ppermute | solution.py:53
  123.9 4.0 %collective-permute-done.30.g1 = f32[8,5632]{1,0:T(8,128)S(1)} collective-permute-done((f32[8,5632]{1,0:T(8,128)S(1)}, f32[8,5632]{1,0:T(8,128)S(1)}, u32[]{:S(2)}, u32[]{:S(2)}) %collective-permute-start.30) | collective-permute-done | bytes 180256 | tf_op jit(solution)/shard_map/ppermute | solution.py:53
  128.9 2.4 %collective-permute-start.33 = (f32[8,1024]{1,0:T(8,128)S(1)}, f32[8,1024]{1,0:T(8,128)S(1)}, u32[]{:S(2)}, u32[]{:S(2)}) collective-permute-start(f32[8,1024]{1,0:T(8,128)S(1)} %get-tuple-element.149.refs_0_), channel_id=1, source_target_pairs={{2,0},{33,1},{4,2},{35,3},{6,4},{37,5},{0,6},{39,7},{10,8},{41,9},... | collective-permute-start | bytes 98312 | tf_op jit(solution)/shard_map/ppermute | solution.py:53
  131.3 2.2 %collective-permute-start.34 = (f32[8,1024]{1,0:T(8,128)S(1)}, f32[8,1024]{1,0:T(8,128)S(1)}, u32[]{:S(2)}, u32[]{:S(2)}) collective-permute-start(f32[8,1024]{1,0:T(8,128)S(1)} %get-tuple-element.149.refs_0_), channel_id=1, source_target_pairs={{4,0},{65,1},{6,2},{67,3},{0,4},{69,5},{2,6},{71,7},{12,8},{73,9},... | collective-permute-start | bytes 98312 | tf_op jit(solution)/shard_map/ppermute | solution.py:53
  133.5 2.5 %collective-permute-start.35 = (f32[8,1024]{1,0:T(8,128)S(1)}, f32[8,1024]{1,0:T(8,128)S(1)}, u32[]{:S(2)}, u32[]{:S(2)}) collective-permute-start(f32[8,1024]{1,0:T(8,128)S(1)} %get-tuple-element.149.refs_0_), channel_id=1, source_target_pairs={{6,0},{97,1},{0,2},{99,3},{2,4},{101,5},{4,6},{103,7},{14,8},{105,... | collective-permute-start | bytes 98312 | tf_op jit(solution)/shard_map/ppermute | solution.py:53
  136.0 1.9 %collective-permute-start.36 = (f32[8,128]{1,0:T(8,128)S(1)}, f32[8,128]{1,0:T(8,128)S(1)}, u32[]{:S(2)}, u32[]{:S(2)}) collective-permute-start(f32[8,128]{1,0:T(8,128)S(1)} %get-tuple-element.147), channel_id=1, source_target_pairs={{0,0},{1,16},{2,32},{3,17},{4,64},{5,18},{6,96},{7,19},{8,1},{9,20... | collective-permute-start | bytes 12296 | tf_op jit(solution)/shard_map/ppermute | solution.py:528
  137.9 9.6 %collective-permute-done.36 = f32[8,128]{1,0:T(8,128)S(1)} collective-permute-done((f32[8,128]{1,0:T(8,128)S(1)}, f32[8,128]{1,0:T(8,128)S(1)}, u32[]{:S(2)}, u32[]{:S(2)}) %collective-permute-start.36) | collective-permute-done | bytes 4128 | tf_op jit(solution)/shard_map/ppermute | solution.py:528
  149.0 2.4 %finish.1 = (f32[64,1024]{1,0:T(8,128)}, f32[1,64]{1,0:T(1,128)}, f32[1,128]{1,0:T(1,128)}) custom-call(s32[7]{0:T(128)S(1)} %stack.55.where, f32[4,8,1024]{2,1,0:T(8,128)S(1)} %collect.3.own, f32[4,8,1024]{2,1,0:T(8,128)S(1)} %collective-permute-done.37.oth, s32[1024,64]{1,0:T(8,128)S(1)} %copy.24.labels, f32[1,64]{1,0:T(1,128)S(1)} %bitcast.45, ...), custom_call_target="tpu_custom_call" | custom-call | flops 1000000 | tf_op jit(solution)/shard_map/finish/pallas_call | solution.py:238
  (95 shorter events, 30.1 us)
Async XLA Ops:
  0.6 7.6 %collective-permute-start = (bf16[128,288]{0,1:T(8,128)(2,1)}, bf16[128,288]{0,1:T(8,128)(2,1)S(1)}, u32[]{:S(2)}, u32[]{:S(2)}) collective-permute-start(bf16[128,288]{0,1:T(8,128)(2,1)} %param.9), channel_id=1, source_target_pairs={{8,0},{9,1},{10,2},{11,3},{12,4},{13,5},{14,6},{15,7},{16,8},{17,9... | collective-permute-start | bytes 221192 | tf_op jit(solution)/shard_map/ppermute | solution.py:53
  4.7 6.3 %collective-permute-start.1 = (bf16[128,288]{0,1:T(8,128)(2,1)}, bf16[128,288]{0,1:T(8,128)(2,1)S(1)}, u32[]{:S(2)}, u32[]{:S(2)}) collective-permute-start(bf16[128,288]{0,1:T(8,128)(2,1)} %param.9), channel_id=1, source_target_pairs={{16,0},{17,1},{18,2},{19,3},{20,4},{21,5},{22,6},{23,7},{24,8},{25... | collective-permute-start | bytes 221192 | tf_op jit(solution)/shard_map/ppermute | solution.py:53
  4.7 6.7 %collective-permute-start.2 = (bf16[128,288]{0,1:T(8,128)(2,1)}, bf16[128,288]{0,1:T(8,128)(2,1)S(1)}, u32[]{:S(2)}, u32[]{:S(2)}) collective-permute-start(bf16[128,288]{0,1:T(8,128)(2,1)} %param.9), channel_id=1, source_target_pairs={{24,0},{25,1},{26,2},{27,3},{28,4},{29,5},{30,6},{31,7},{0,8},{1,9... | collective-permute-start | bytes 221192 | tf_op jit(solution)/shard_map/ppermute | solution.py:53
  11.9 11.6 %collective-permute-start.3 = (bf16[128,1152]{1,0:T(8,128)(2,1)S(1)}, bf16[128,1152]{1,0:T(8,128)(2,1)S(1)}, u32[]{:S(2)}, u32[]{:S(2)}) collective-permute-start(bf16[128,1152]{1,0:T(8,128)(2,1)S(1)} %settle.1.refs_0_), channel_id=1, source_target_pairs={{32,0},{3,1},{34,2},{5,3},{36,4},{7,5},{38,6},{1,7},{40,8},{11,9},... | collective-permute-start | bytes 884744 | tf_op jit(solution)/shard_map/ppermute | solution.py:53
  12.7 10.8 %collective-permute-start.4 = (bf16[128,1152]{1,0:T(8,128)(2,1)S(1)}, bf16[128,1152]{1,0:T(8,128)(2,1)S(1)}, u32[]{:S(2)}, u32[]{:S(2)}) collective-permute-start(bf16[128,1152]{1,0:T(8,128)(2,1)S(1)} %settle.1.refs_0_), channel_id=1, source_target_pairs={{64,0},{5,1},{66,2},{7,3},{68,4},{1,5},{70,6},{3,7},{72,8},{13,9},... | collective-permute-start | bytes 884744 | tf_op jit(solution)/shard_map/ppermute | solution.py:53
  13.6 10.3 %collective-permute-start.5 = (bf16[128,1152]{1,0:T(8,128)(2,1)S(1)}, bf16[128,1152]{1,0:T(8,128)(2,1)S(1)}, u32[]{:S(2)}, u32[]{:S(2)}) collective-permute-start(bf16[128,1152]{1,0:T(8,128)(2,1)S(1)} %settle.1.refs_0_), channel_id=1, source_target_pairs={{96,0},{7,1},{98,2},{1,3},{100,4},{3,5},{102,6},{5,7},{104,8},{15,... | collective-permute-start | bytes 884744 | tf_op jit(solution)/shard_map/ppermute | solution.py:53
  24.1 16.3 %collective-permute-start.6 = (bf16[4,128,1152]{2,1,0:T(8,128)(2,1)S(1)}, bf16[4,128,1152]{2,1,0:T(8,128)(2,1)S(1)}, u32[]{:S(2)}, u32[]{:S(2)}) collective-permute-start(bf16[4,128,1152]{2,1,0:T(8,128)(2,1)S(1)} %collect.2.refs_0_.block), channel_id=1, source_target_pairs={{2,0},{33,1},{4,2},{35,3},{6,4},{37,5},{0,6},{39,7},{10,8},{41,9},... | collective-permute-start | bytes 3538952 | tf_op jit(solution)/shard_map/ppermute | solution.py:53
  24.7 16.9 %collective-permute-start.7 = (bf16[4,128,1152]{2,1,0:T(8,128)(2,1)S(1)}, bf16[4,128,1152]{2,1,0:T(8,128)(2,1)S(1)}, u32[]{:S(2)}, u32[]{:S(2)}) collective-permute-start(bf16[4,128,1152]{2,1,0:T(8,128)(2,1)S(1)} %collect.2.refs_0_.block), channel_id=1, source_target_pairs={{6,0},{97,1},{0,2},{99,3},{2,4},{101,5},{4,6},{103,7},{14,8},{105,... | collective-permute-start | bytes 3538952 | tf_op jit(solution)/shard_map/ppermute | solution.py:53
  41.6 4.0 %collective-permute-start.12 = (bf16[4,128,1152]{2,1,0:T(8,128)(2,1)S(1)}, bf16[4,128,1152]{2,1,0:T(8,128)(2,1)S(1)}, u32[]{:S(2)}, u32[]{:S(2)}) collective-permute-start(bf16[4,128,1152]{2,1,0:T(8,128)(2,1)S(1)} %collective-permute-done.6.a.refs_0_.side1), channel_id=1, source_target_pairs={{0,1},{1,0},{2,3},{3,2},{4,5},{5,4},{6,7},{7,6},{8,9},{9,8},{10,11... | collective-permute-start | bytes 3538952 | tf_op jit(solution)/shard_map/ppermute | solution.py:58
  41.6 8.9 %collective-permute-start.11 = (bf16[4,128,1152]{2,1,0:T(8,128)(2,1)S(1)}, bf16[4,128,1152]{2,1,0:T(8,128)(2,1)S(1)}, u32[]{:S(2)}, u32[]{:S(2)}) collective-permute-start(bf16[4,128,1152]{2,1,0:T(8,128)(2,1)S(1)} %collective-permute-done.7.b.refs_0_.side3), channel_id=1, source_target_pairs={{0,1},{1,0},{2,3},{3,2},{4,5},{5,4},{6,7},{7,6},{8,9},{9,8},{10,11... | collective-permute-start | bytes 3538952 | tf_op jit(solution)/shard_map/ppermute | solution.py:58
  42.2 13.2 %collective-permute-start.10 = (bf16[2,128,1152]{2,1,0:T(8,128)(2,1)S(1)}, bf16[2,128,1152]{2,1,0:T(8,128)(2,1)S(1)}, u32[]{:S(2)}, u32[]{:S(2)}) collective-permute-start(bf16[2,128,1152]{2,1,0:T(8,128)(2,1)S(1)} %get-tuple-element.96), channel_id=1, source_target_pairs={{6,0},{97,1},{0,2},{99,3},{2,4},{101,5},{4,6},{103,7},{14,8},{105,... | collective-permute-start | bytes 1769480 | tf_op jit(solution)/shard_map/ppermute | solution.py:53
  43.1 12.4 %collective-permute-start.9 = (bf16[2,128,1152]{2,1,0:T(8,128)(2,1)S(1)}, bf16[2,128,1152]{2,1,0:T(8,128)(2,1)S(1)}, u32[]{:S(2)}, u32[]{:S(2)}) collective-permute-start(bf16[2,128,1152]{2,1,0:T(8,128)(2,1)S(1)} %get-tuple-element.95), channel_id=1, source_target_pairs={{2,0},{33,1},{4,2},{35,3},{6,4},{37,5},{0,6},{39,7},{10,8},{41,9},... | collective-permute-start | bytes 1769480 | tf_op jit(solution)/shard_map/ppermute | solution.py:53
  55.5 3.6 %collective-permute-start.13 = (bf16[2,128,1152]{2,1,0:T(8,128)(2,1)S(1)}, bf16[2,128,1152]{2,1,0:T(8,128)(2,1)S(1)}, u32[]{:S(2)}, u32[]{:S(2)}) collective-permute-start(bf16[2,128,1152]{2,1,0:T(8,128)(2,1)S(1)} %collective-permute-done.9.refs_0_.low), channel_id=1, source_target_pairs={{0,1},{1,0},{2,3},{3,2},{4,5},{5,4},{6,7},{7,6},{8,9},{9,8},{10,11... | collective-permute-start | bytes 1769480 | tf_op jit(solution)/shard_map/ppermute | solution.py:58
  55.5 3.5 %collective-permute-start.14 = (bf16[2,128,1152]{2,1,0:T(8,128)(2,1)S(1)}, bf16[2,128,1152]{2,1,0:T(8,128)(2,1)S(1)}, u32[]{:S(2)}, u32[]{:S(2)}) collective-permute-start(bf16[2,128,1152]{2,1,0:T(8,128)(2,1)S(1)} %collective-permute-done.10.refs_1_.high), channel_id=1, source_target_pairs={{0,1},{1,0},{2,3},{3,2},{4,5},{5,4},{6,7},{7,6},{8,9},{9,8},{10,11... | collective-permute-start | bytes 1769480 | tf_op jit(solution)/shard_map/ppermute | solution.py:58
  65.4 3.0 %collective-permute-start.16 = (bf16[128,2432]{1,0:T(8,128)(2,1)S(1)}, bf16[128,2432]{1,0:T(8,128)(2,1)S(1)}, u32[]{:S(2)}, u32[]{:S(2)}) collective-permute-start(bf16[128,2432]{1,0:T(8,128)(2,1)S(1)} %get-tuple-element.111), channel_id=1, source_target_pairs={{0,1},{1,0},{2,3},{3,2},{4,5},{5,4},{6,7},{7,6},{8,9},{9,8},{10,11... | collective-permute-start | bytes 1867784 | tf_op jit(solution)/shard_map/ppermute | solution.py:58
  68.9 11.6 %collective-permute-start.17 = (bf16[64,4992]{1,0:T(8,128)(2,1)S(1)}, bf16[64,4992]{1,0:T(8,128)(2,1)S(1)}, u32[]{:S(2)}, u32[]{:S(2)}) collective-permute-start(bf16[64,4992]{1,0:T(8,128)(2,1)S(1)} %get-tuple-element.116), channel_id=1, source_target_pairs={{6,0},{97,1},{0,2},{99,3},{2,4},{101,5},{4,6},{103,7},{14,8},{105,... | collective-permute-start | bytes 1916936 | tf_op jit(solution)/shard_map/ppermute | solution.py:53
  69.5 11.6 %collective-permute-start.18 = (bf16[64,4992]{1,0:T(8,128)(2,1)S(1)}, bf16[64,4992]{1,0:T(8,128)(2,1)S(1)}, u32[]{:S(2)}, u32[]{:S(2)}) collective-permute-start(bf16[64,4992]{1,0:T(8,128)(2,1)S(1)} %get-tuple-element.117), channel_id=1, source_target_pairs={{2,0},{33,1},{4,2},{35,3},{6,4},{37,5},{0,6},{39,7},{10,8},{41,9},... | collective-permute-start | bytes 1916936 | tf_op jit(solution)/shard_map/ppermute | solution.py:53
  75.6 6.6 %collective-permute-start.22 = (bf16[128,2432]{1,0:T(8,128)(2,1)S(1)}, bf16[128,2432]{1,0:T(8,128)(2,1)S(1)}, u32[]{:S(2)}, u32[]{:S(2)}) collective-permute-start(bf16[128,2432]{1,0:T(8,128)(2,1)S(1)} %get-tuple-element.129), channel_id=1, source_target_pairs={{0,1},{1,0},{2,3},{3,2},{4,5},{5,4},{6,7},{7,6},{8,9},{9,8},{10,11... | collective-permute-start | bytes 1867784 | tf_op jit(solution)/shard_map/ppermute | solution.py:58
  79.1 3.9 %collective-permute-start.20 = (bf16[128,2432]{1,0:T(8,128)(2,1)S(1)}, bf16[128,2432]{1,0:T(8,128)(2,1)S(1)}, u32[]{:S(2)}, u32[]{:S(2)}) collective-permute-start(bf16[128,2432]{1,0:T(8,128)(2,1)S(1)} %get-tuple-element.125), channel_id=1, source_target_pairs={{0,1},{1,0},{2,3},{3,2},{4,5},{5,4},{6,7},{7,6},{8,9},{9,8},{10,11... | collective-permute-start | bytes 1867784 | tf_op jit(solution)/shard_map/ppermute | solution.py:58
  83.7 17.8 %collective-permute-start.25 = (bf16[128,4736]{1,0:T(8,128)(2,1)S(1)}, bf16[128,4736]{1,0:T(8,128)(2,1)S(1)}, u32[]{:S(2)}, u32[]{:S(2)}) collective-permute-start(bf16[128,4736]{1,0:T(8,128)(2,1)S(1)} %pair_sum.4), channel_id=1, source_target_pairs={{6,0},{97,1},{0,2},{99,3},{2,4},{101,5},{4,6},{103,7},{14,8},{105,... | collective-permute-start | bytes 3637256 | tf_op jit(solution)/shard_map/ppermute | solution.py:53
  84.6 17.8 %collective-permute-start.26 = (bf16[128,4736]{1,0:T(8,128)(2,1)S(1)}, bf16[128,4736]{1,0:T(8,128)(2,1)S(1)}, u32[]{:S(2)}, u32[]{:S(2)}) collective-permute-start(bf16[128,4736]{1,0:T(8,128)(2,1)S(1)} %pair_sum.5), channel_id=1, source_target_pairs={{2,0},{33,1},{4,2},{35,3},{6,4},{37,5},{0,6},{39,7},{10,8},{41,9},... | collective-permute-start | bytes 3637256 | tf_op jit(solution)/shard_map/ppermute | solution.py:53
  90.5 3.0 %collective-permute-start.24 = (bf16[128,2432]{1,0:T(8,128)(2,1)S(1)}, bf16[128,2432]{1,0:T(8,128)(2,1)S(1)}, u32[]{:S(2)}, u32[]{:S(2)}) collective-permute-start(bf16[128,2432]{1,0:T(8,128)(2,1)S(1)} %get-tuple-element.135), channel_id=1, source_target_pairs={{0,1},{1,0},{2,3},{3,2},{4,5},{5,4},{6,7},{7,6},{8,9},{9,8},{10,11... | collective-permute-start | bytes 1867784 | tf_op jit(solution)/shard_map/ppermute | solution.py:58
  103.8 10.8 %collective-permute-start.27 = (bf16[32,5120]{1,0:T(8,128)(2,1)S(1)}, bf16[32,5120]{1,0:T(8,128)(2,1)S(1)}, u32[]{:S(2)}, u32[]{:S(2)}) collective-permute-start(bf16[32,5120]{1,0:T(8,128)(2,1)S(1)} %get-tuple-element.139), channel_id=1, source_target_pairs={{96,0},{25,1},{98,2},{27,3},{100,4},{29,5},{102,6},{31,7},{104,8},... | collective-permute-start | bytes 983048 | tf_op jit(solution)/shard_map/ppermute | solution.py:53
  106.5 8.7 %collective-permute-start.28 = (bf16[32,5120]{1,0:T(8,128)(2,1)S(1)}, bf16[32,5120]{1,0:T(8,128)(2,1)S(1)}, u32[]{:S(2)}, u32[]{:S(2)}) collective-permute-start(bf16[32,5120]{1,0:T(8,128)(2,1)S(1)} %get-tuple-element.140), channel_id=1, source_target_pairs={{64,0},{17,1},{66,2},{19,3},{68,4},{21,5},{70,6},{23,7},{72,8},{25... | collective-permute-start | bytes 983048 | tf_op jit(solution)/shard_map/ppermute | solution.py:53
  106.5 11.8 %collective-permute-start.29 = (bf16[32,5120]{1,0:T(8,128)(2,1)S(1)}, bf16[32,5120]{1,0:T(8,128)(2,1)S(1)}, u32[]{:S(2)}, u32[]{:S(2)}) collective-permute-start(bf16[32,5120]{1,0:T(8,128)(2,1)S(1)} %get-tuple-element.141), channel_id=1, source_target_pairs={{32,0},{9,1},{34,2},{11,3},{36,4},{13,5},{38,6},{15,7},{40,8},{17,... | collective-permute-start | bytes 983048 | tf_op jit(solution)/shard_map/ppermute | solution.py:53
  119.2 8.7 %collective-permute-start.30 = (f32[8,5632]{1,0:T(8,128)S(1)}, f32[8,5632]{1,0:T(8,128)S(1)}, u32[]{:S(2)}, u32[]{:S(2)}) collective-permute-start(f32[8,5632]{1,0:T(8,128)S(1)} %get-tuple-element.143), channel_id=1, source_target_pairs={{24,0},{7,1},{26,2},{1,3},{28,4},{3,5},{30,6},{5,7},{0,8},{15,9},{... | collective-permute-start | bytes 540680 | tf_op jit(solution)/shard_map/ppermute | solution.py:53
  119.3 8.6 %collective-permute-start.31 = (f32[8,5632]{1,0:T(8,128)S(1)}, f32[8,5632]{1,0:T(8,128)S(1)}, u32[]{:S(2)}, u32[]{:S(2)}) collective-permute-start(f32[8,5632]{1,0:T(8,128)S(1)} %get-tuple-element.144), channel_id=1, source_target_pairs={{16,0},{5,1},{18,2},{7,3},{20,4},{1,5},{22,6},{3,7},{24,8},{13,9},... | collective-permute-start | bytes 540680 | tf_op jit(solution)/shard_map/ppermute | solution.py:53
  121.6 7.2 %collective-permute-start.32 = (f32[8,5632]{1,0:T(8,128)S(1)}, f32[8,5632]{1,0:T(8,128)S(1)}, u32[]{:S(2)}, u32[]{:S(2)}) collective-permute-start(f32[8,5632]{1,0:T(8,128)S(1)} %get-tuple-element.145), channel_id=1, source_target_pairs={{8,0},{3,1},{10,2},{5,3},{12,4},{7,5},{14,6},{1,7},{16,8},{11,9},{... | collective-permute-start | bytes 540680 | tf_op jit(solution)/shard_map/ppermute | solution.py:53
  128.9 18.6 %collective-permute-start.33 = (f32[8,1024]{1,0:T(8,128)S(1)}, f32[8,1024]{1,0:T(8,128)S(1)}, u32[]{:S(2)}, u32[]{:S(2)}) collective-permute-start(f32[8,1024]{1,0:T(8,128)S(1)} %get-tuple-element.149.refs_0_), channel_id=1, source_target_pairs={{2,0},{33,1},{4,2},{35,3},{6,4},{37,5},{0,6},{39,7},{10,8},{41,9},... | collective-permute-start | bytes 98312 | tf_op jit(solution)/shard_map/ppermute | solution.py:53
  131.3 16.2 %collective-permute-start.34 = (f32[8,1024]{1,0:T(8,128)S(1)}, f32[8,1024]{1,0:T(8,128)S(1)}, u32[]{:S(2)}, u32[]{:S(2)}) collective-permute-start(f32[8,1024]{1,0:T(8,128)S(1)} %get-tuple-element.149.refs_0_), channel_id=1, source_target_pairs={{4,0},{65,1},{6,2},{67,3},{0,4},{69,5},{2,6},{71,7},{12,8},{73,9},... | collective-permute-start | bytes 98312 | tf_op jit(solution)/shard_map/ppermute | solution.py:53
  133.5 14.1 %collective-permute-start.35 = (f32[8,1024]{1,0:T(8,128)S(1)}, f32[8,1024]{1,0:T(8,128)S(1)}, u32[]{:S(2)}, u32[]{:S(2)}) collective-permute-start(f32[8,1024]{1,0:T(8,128)S(1)} %get-tuple-element.149.refs_0_), channel_id=1, source_target_pairs={{6,0},{97,1},{0,2},{99,3},{2,4},{101,5},{4,6},{103,7},{14,8},{105,... | collective-permute-start | bytes 98312 | tf_op jit(solution)/shard_map/ppermute | solution.py:53
  136.0 11.5 %collective-permute-start.36 = (f32[8,128]{1,0:T(8,128)S(1)}, f32[8,128]{1,0:T(8,128)S(1)}, u32[]{:S(2)}, u32[]{:S(2)}) collective-permute-start(f32[8,128]{1,0:T(8,128)S(1)} %get-tuple-element.147), channel_id=1, source_target_pairs={{0,0},{1,16},{2,32},{3,17},{4,64},{5,18},{6,96},{7,19},{8,1},{9,20... | collective-permute-start | bytes 12296 | tf_op jit(solution)/shard_map/ppermute | solution.py:528
  (12 other events, 101.3 us)
where the time goes:
time: 152 us; the launch traced here: 151 us
  waiting for transfers between devices  56.3 us (37%)
  Pallas kernels  49.3 us (32%)
  starting transfers between devices  41.3 us (27%)
  local copies, waits for them, and re-layouts  3.3 us (2%)
    ppermute x23, waiting for transfers between devices, pull(): return lax.ppermute(value, AXES, pull_perm(axis0, axis1, step))  39.4 us
    ppermute x23, starting transfers between devices, pull(): return lax.ppermute(value, AXES, pull_perm(axis0, axis1, step))  36.2 us
    pallas_call x5, Pallas kernels, encode(): pl.pallas_call(functools.partial(encode_kernel, stage, which, 256), in_sp...  20.5 us
    pallas_call x4, Pallas kernels, decode(): pl.pallas_call(functools.partial(decode_kernel, step, 768), in_specs=[pl....  13.6 us
    ppermute x1, waiting for transfers between devices, on_device(): err = lax.ppermute(err, AXES, owners)  9.59 us
    pallas_call x2, Pallas kernels, load(): pl.pallas_call(load_kernel, in_specs=[pl.BlockSpec(memory_space=pltpu.HBM...  7.6 us
    pallas_call x12, Pallas kernels, small_call(): pl.pallas_call(kernel, in_specs=[smem] * scalars + [vmem] * (len(args) -...  7.56 us
    ppermute x14, waiting for transfers between devices, swap(): return lax.ppermute(value, AXES, pairs)  7.31 us
  transfers between devices with their start and end apart: 38, of which 21 were waited for; matrix products, arithmetic and copies ran while one was open for 2% of the time, Pallas kernels for 24%

commit v1 on v0

--- a/solution.py
+++ b/solution.py
@@ -115,10 +115,17 @@
         gate = jax.nn.sigmoid((preact - cutoff) / softness)
         return (preact * gate).astype(BF16)
 
-    def tiles(work):
+    def tiles(*works):
+        if stage == STAGES[-1]:
+            for n in range(enc.shape[1] // tile):
+                for work in works:
+                    work(slice(tile * n, tile * (n + 1)))
+            return
+
         @pl.loop(0, enc.shape[1] // tile)
         def _(n):
-            work(pl.ds(pl.multiple_of(n * tile, tile), tile))
+            for work in works:
+                work(pl.ds(pl.multiple_of(n * tile, tile), tile))
 
     def few(parts):
         def work(cols):
@@ -130,7 +137,7 @@
             )
             xa[:, cols] = activate(pre, cols)
 
-        tiles(work)
+        return work
 
     def many(parts):
         def work(cols):
@@ -148,19 +155,18 @@
                 else:
                     ya[span, cols] = part
 
-        tiles(work)
+        return work
 
     for turn in (0, 1):
 
         @pl.when(core == turn)
         def _(turn=turn):
             if which is None:
-                few([blocks[turn]])
-                many([blocks[1 - turn]])
+                tiles(few([blocks[turn]]), many([blocks[1 - turn]]))
             elif which == turn:
-                few(blocks)
+                tiles(few(blocks))
             else:
-                many(blocks)
+                tiles(many(blocks))
 
 
 def encode(stage, which, where, blocks, enc, bias, cut, acc, done=()):
@@ -209,6 +215,17 @@
     keep[:, D:] = logits[:128]
     send1[:, C:] = logits[128:]
 
+    if step == 0:
+        for i, send in enumerate((send0, send1)):
+
+            @pl.loop(0, C // tile)
+            def _(n, i=i, send=send):
+                cols = pl.ds(pl.multiple_of(C * i + n * tile, tile), tile)
+                out = jnp.dot(lhs[...], dec[:, cols], preferred_element_type=F32).astype(BF16)
+                keep[:, cols] = out[:128]
+                send[:, pl.ds(pl.multiple_of(n * tile, tile), tile)] = out[128:]
+
+        return
     for n in range(D // tile):
         cols = slice(tile * n, tile * (n + 1))
         send, start = (send0, tile * n) if tile * n < C else (send1, tile * n - C)

time: 152 us -> 150 us (0.987)
  Pallas kernels: 49.3 us -> 46.9 us
    pallas_call x5, Pallas kernels: 20.5 us -> 17.2 us  [encode(): pl.pallas_call(functools.partial(encode_kernel, stage, which, 256), in_sp...]
  transfers between devices with their start and end apart: 38 -> 38, of which waited for: 21 -> 22; matrix products, arithmetic and copies ran while one was open for 2% -> 2% of each run, Pallas kernels for 24% -> 23%
where the time goes in v1:
time: 150 us; the launch traced here: 149 us
  waiting for transfers between devices  56.3 us (38%)
  Pallas kernels  46.9 us (31%)
  starting transfers between devices  41.3 us (28%)
  local copies, waits for them, and re-layouts  3.3 us (2%)
    ppermute x23, waiting for transfers between devices, pull(): return lax.ppermute(value, AXES, pull_perm(axis0, axis1, step))  40.2 us
    ppermute x23, starting transfers between devices, pull(): return lax.ppermute(value, AXES, pull_perm(axis0, axis1, step))  36 us
    pallas_call x5, Pallas kernels, encode(): pl.pallas_call(functools.partial(encode_kernel, stage, which, 256), in_sp...  17.2 us
    pallas_call x4, Pallas kernels, decode(): pl.pallas_call(functools.partial(decode_kernel, step, 768), in_specs=[pl....  14.6 us
    ppermute x1, waiting for transfers between devices, on_device(): err = lax.ppermute(err, AXES, owners)  9.59 us
    pallas_call x2, Pallas kernels, load(): pl.pallas_call(load_kernel, in_specs=[pl.BlockSpec(memory_space=pltpu.HBM...  7.6 us
    pallas_call x12, Pallas kernels, small_call(): pl.pallas_call(kernel, in_specs=[smem] * scalars + [vmem] * (len(args) -...  7.56 us
    ppermute x14, waiting for transfers between devices, swap(): return lax.ppermute(value, AXES, pairs)  6.45 us
  transfers between devices with their start and end apart: 38, of which 22 were waited for; matrix products, arithmetic and copies ran while one was open for 2% of the time, Pallas kernels for 23%

profile of v1, /device:TPU:26, one launch (start us, length us, event | category | flops | bytes accessed | tf_op | source)
XLA Modules:
  0.0 149.0 jit_solution(11636897388859179633)
XLA Ops:
  0.6 4.1 %collective-permute-start = (bf16[128,288]{0,1:T(8,128)(2,1)}, bf16[128,288]{0,1:T(8,128)(2,1)S(1)}, u32[]{:S(2)}, u32[]{:S(2)}) collective-permute-start(bf16[128,288]{0,1:T(8,128)(2,1)} %param.9), channel_id=1, source_target_pairs={{8,0},{9,1},{10,2},{11,3},{12,4},{13,5},{14,6},{15,7},{16,8},{17,9... | collective-permute-start | bytes 221192 | tf_op jit(solution)/shard_map/ppermute | solution.py:53
  8.3 2.7 %collective-permute-done.1 = bf16[128,288]{0,1:T(8,128)(2,1)S(1)} collective-permute-done((bf16[128,288]{0,1:T(8,128)(2,1)}, bf16[128,288]{0,1:T(8,128)(2,1)S(1)}, u32[]{:S(2)}, u32[]{:S(2)}) %collective-permute-start.1) | collective-permute-done | bytes 73760 | tf_op jit(solution)/shard_map/ppermute | solution.py:53
  13.6 2.2 %collective-permute-start.5 = (bf16[128,1152]{1,0:T(8,128)(2,1)S(1)}, bf16[128,1152]{1,0:T(8,128)(2,1)S(1)}, u32[]{:S(2)}, u32[]{:S(2)}) collective-permute-start(bf16[128,1152]{1,0:T(8,128)(2,1)S(1)} %settle.1.refs_0_), channel_id=1, source_target_pairs={{96,0},{7,1},{98,2},{1,3},{100,4},{3,5},{102,6},{5,7},{104,8},{15,... | collective-permute-start | bytes 884744 | tf_op jit(solution)/shard_map/ppermute | solution.py:53
  15.8 3.8 %load.2.refs_2_ = bf16[4608,1024]{1,0:T(8,128)(2,1)S(1)} custom-call(bf16[4608,1024]{1,0:T(8,128)(2,1)} %source), custom_call_target="tpu_custom_call" | custom-call | flops 1000000 | tf_op jit(solution)/shard_map/load/pallas_call | solution.py:80
  19.6 3.8 %load.3.dec = bf16[1024,4608]{1,0:T(8,128)(2,1)S(1)} custom-call(bf16[1024,4608]{1,0:T(8,128)(2,1)} %source.1), custom_call_target="tpu_custom_call" | custom-call | flops 1000000 | tf_op jit(solution)/shard_map/load/pallas_call | solution.py:80
  26.9 4.1 %encode.5 = (bf16[128,1024]{1,0:T(8,128)(2,1)S(1)}, f32[512,1024]{1,0:T(8,128)S(1)}) custom-call(s32[7]{0:T(128)S(1)} %stack.55.where, bf16[4,128,1152]{2,1,0:T(8,128)(2,1)S(1)} %collect.2.refs_0_.block, bf16[4,128,1152]{2,1,0:T(8,128)(2,1)S(1)} %collective-permute-done.8.refs_1_, bf16[4608,1024]{1,0:T(8,128)(2,1)S(1)} %load.2.refs_2_, ...), custom_call_target="tpu_custom_call" | custom-call | flops 1000000 | tf_op jit(solution)/shard_map/encode/pallas_call | solution.py:184
  31.1 9.3 %collective-permute-done.6.a.refs_0_.side1 = bf16[4,128,1152]{2,1,0:T(8,128)(2,1)S(1)} collective-permute-done((bf16[4,128,1152]{2,1,0:T(8,128)(2,1)S(1)}, bf16[4,128,1152]{2,1,0:T(8,128)(2,1)S(1)}, u32[]{:S(2)}, u32[]{:S(2)}) %collective-permute-start.6) | collective-permute-done | bytes 1179680 | tf_op jit(solution)/shard_map/ppermute | solution.py:53
  43.1 2.6 %collective-permute-start.9 = (bf16[2,128,1152]{2,1,0:T(8,128)(2,1)S(1)}, bf16[2,128,1152]{2,1,0:T(8,128)(2,1)S(1)}, u32[]{:S(2)}, u32[]{:S(2)}) collective-permute-start(bf16[2,128,1152]{2,1,0:T(8,128)(2,1)S(1)} %get-tuple-element.95), channel_id=1, source_target_pairs={{2,0},{33,1},{4,2},{35,3},{6,4},{37,5},{0,6},{39,7},{10,8},{41,9},... | collective-permute-start | bytes 1769480 | tf_op jit(solution)/shard_map/ppermute | solution.py:53
  45.6 4.2 %encode.6 = (bf16[128,1024]{1,0:T(8,128)(2,1)S(1)}, f32[512,1024]{1,0:T(8,128)S(1)}) custom-call(s32[7]{0:T(128)S(1)} %stack.55.where, bf16[4,128,1152]{2,1,0:T(8,128)(2,1)S(1)} %collective-permute-done.6.a.refs_0_.side1, bf16[4,128,1152]{2,1,0:T(8,128)(2,1)S(1)} %collective-permute-done.12.refs_1_, ...), custom_call_target="tpu_custom_call", output_to_operand_aliasing={{1}: (6, {})} | custom-call | flops 1000000 | tf_op jit(solution)/shard_map/encode/pallas_call | solution.py:184
  49.8 4.2 %encode.7 = (bf16[128,1024]{1,0:T(8,128)(2,1)S(1)}, f32[512,1024]{1,0:T(8,128)S(1)}) custom-call(s32[7]{0:T(128)S(1)} %stack.55.where, bf16[4,128,1152]{2,1,0:T(8,128)(2,1)S(1)} %collective-permute-done.7.b.refs_0_.side3, bf16[4,128,1152]{2,1,0:T(8,128)(2,1)S(1)} %collective-permute-done.11.refs_1_, ...), custom_call_target="tpu_custom_call", output_to_operand_aliasing={{1}: (6, {})} | custom-call | flops 1000000 | tf_op jit(solution)/shard_map/encode/pallas_call | solution.py:184
  54.6 2.3 %encode.8 = (bf16[128,1024]{1,0:T(8,128)(2,1)S(1)}, bf16[512,1024]{1,0:T(8,128)(2,1)S(1)}) custom-call(s32[7]{0:T(128)S(1)} %stack.55.where, bf16[2,128,1152]{2,1,0:T(8,128)(2,1)S(1)} %collective-permute-done.9.refs_0_.low, bf16[2,128,1152]{2,1,0:T(8,128)(2,1)S(1)} %collective-permute-done.10.refs_1_.high, bf16[4608,1024]{1,0:T(8,128)(2,1)S(1)} %load.2.refs_2_, ...), custom_call_target="tpu_custom_call" | custom-call | flops 1000000 | tf_op jit(solution)/shard_map/encode/pallas_call | solution.py:184
  57.1 2.4 %encode.9 = (bf16[128,1024]{1,0:T(8,128)(2,1)S(1)}, bf16[512,1024]{1,0:T(8,128)(2,1)S(1)}) custom-call(s32[7]{0:T(128)S(1)} %stack.55.where, bf16[2,128,1152]{2,1,0:T(8,128)(2,1)S(1)} %collective-permute-done.13.refs_0_, bf16[2,128,1152]{2,1,0:T(8,128)(2,1)S(1)} %collective-permute-done.14.refs_1_, ...), custom_call_target="tpu_custom_call", output_to_operand_aliasing={{0}: (7, {}), {1}: (8, {})} | custom-call | flops 1000000 | tf_op jit(solution)/shard_map/encode/pallas_call | solution.py:184
  59.5 3.4 %decode.4 = (bf16[128,4736]{1,0:T(8,128)(2,1)S(1)}, bf16[128,2304]{1,0:T(8,128)(2,1)S(1)}, bf16[128,2432]{1,0:T(8,128)(2,1)S(1)}) custom-call(s32[7]{0:T(128)S(1)} %stack.55.where, bf16[128,1024]{1,0:T(8,128)(2,1)S(1)} %get-tuple-element.105.xa.refs_2_, bf16[4,128,1024]{2,1,0:T(8,128)(2,1)S(1)} %bitcast.30, bf16[1024,4608]{1,0:T(8,128)(2,1)S(1)} %load.3.dec, ...), custom_call_target="tpu_custom_call" | custom-call | flops 1000000 | tf_op jit(solution)/shard_map/decode/pallas_call | solution.py:240
  63.5 2.4 %collective-permute-done.15.b0 = bf16[128,2304]{1,0:T(8,128)(2,1)S(1)} collective-permute-done((bf16[128,2304]{1,0:T(8,128)(2,1)S(1)}, bf16[128,2304]{1,0:T(8,128)(2,1)S(1)}, u32[]{:S(2)}, u32[]{:S(2)}) %collective-permute-start.15) | collective-permute-done | bytes 589856 | tf_op jit(solution)/shard_map/ppermute | solution.py:58
  66.4 1.9 %collective-permute-start.17 = (bf16[64,4992]{1,0:T(8,128)(2,1)S(1)}, bf16[64,4992]{1,0:T(8,128)(2,1)S(1)}, u32[]{:S(2)}, u32[]{:S(2)}) collective-permute-start(bf16[64,4992]{1,0:T(8,128)(2,1)S(1)} %get-tuple-element.116), channel_id=1, source_target_pairs={{6,0},{97,1},{0,2},{99,3},{2,4},{101,5},{4,6},{103,7},{14,8},{105,... | collective-permute-start | bytes 1916936 | tf_op jit(solution)/shard_map/ppermute | solution.py:53
  69.8 3.4 %decode.6 = (bf16[128,4736]{1,0:T(8,128)(2,1)S(1)}, bf16[128,2304]{1,0:T(8,128)(2,1)S(1)}, bf16[128,2432]{1,0:T(8,128)(2,1)S(1)}) custom-call(s32[7]{0:T(128)S(1)} %stack.55.where, bf16[128,1024]{1,0:T(8,128)(2,1)S(1)} %get-tuple-element.120.xa.refs_3_, bf16[4,128,1024]{2,1,0:T(8,128)(2,1)S(1)} %bitcast.31, bf16[1024,4608]{1,0:T(8,128)(2,1)S(1)} %load.3.dec, ...), custom_call_target="tpu_custom_call" | custom-call | flops 1000000 | tf_op jit(solution)/shard_map/decode/pallas_call | solution.py:240
  73.5 3.4 %decode.5 = (bf16[128,4736]{1,0:T(8,128)(2,1)S(1)}, bf16[128,2304]{1,0:T(8,128)(2,1)S(1)}, bf16[128,2432]{1,0:T(8,128)(2,1)S(1)}) custom-call(s32[7]{0:T(128)S(1)} %stack.55.where, bf16[128,1024]{1,0:T(8,128)(2,1)S(1)} %get-tuple-element.118.xa.refs_1_, bf16[4,128,1024]{2,1,0:T(8,128)(2,1)S(1)} %bitcast.32, bf16[1024,4608]{1,0:T(8,128)(2,1)S(1)} %load.3.dec, ...), custom_call_target="tpu_custom_call" | custom-call | flops 1000000 | tf_op jit(solution)/shard_map/decode/pallas_call | solution.py:240
  81.6 1.8 %collective-permute-start.25 = (bf16[128,4736]{1,0:T(8,128)(2,1)S(1)}, bf16[128,4736]{1,0:T(8,128)(2,1)S(1)}, u32[]{:S(2)}, u32[]{:S(2)}) collective-permute-start(bf16[128,4736]{1,0:T(8,128)(2,1)S(1)} %pair_sum.4), channel_id=1, source_target_pairs={{6,0},{97,1},{0,2},{99,3},{2,4},{101,5},{4,6},{103,7},{14,8},{105,... | collective-permute-start | bytes 3637256 | tf_op jit(solution)/shard_map/ppermute | solution.py:53
  84.9 4.4 %decode.7 = (bf16[128,4736]{1,0:T(8,128)(2,1)S(1)}, bf16[128,2304]{1,0:T(8,128)(2,1)S(1)}, bf16[128,2432]{1,0:T(8,128)(2,1)S(1)}) custom-call(s32[7]{0:T(128)S(1)} %stack.55.where, bf16[128,1024]{1,0:T(8,128)(2,1)S(1)} %get-tuple-element.132.xa.refs_0_, bf16[4,128,1024]{2,1,0:T(8,128)(2,1)S(1)} %bitcast.33, bf16[1024,4608]{1,0:T(8,128)(2,1)S(1)} %load.3.dec, ...), custom_call_target="tpu_custom_call" | custom-call | flops 1000000 | tf_op jit(solution)/shard_map/decode/pallas_call | solution.py:240
  89.9 2.4 %collective-permute-done.23.b0 = bf16[128,2304]{1,0:T(8,128)(2,1)S(1)} collective-permute-done((bf16[128,2304]{1,0:T(8,128)(2,1)S(1)}, bf16[128,2304]{1,0:T(8,128)(2,1)S(1)}, u32[]{:S(2)}, u32[]{:S(2)}) %collective-permute-start.23) | collective-permute-done | bytes 589856 | tf_op jit(solution)/shard_map/ppermute | solution.py:58
  92.3 7.1 %collective-permute-done.25.g1 = bf16[128,4736]{1,0:T(8,128)(2,1)S(1)} collective-permute-done((bf16[128,4736]{1,0:T(8,128)(2,1)S(1)}, bf16[128,4736]{1,0:T(8,128)(2,1)S(1)}, u32[]{:S(2)}, u32[]{:S(2)}) %collective-permute-start.25) | collective-permute-done | bytes 1212448 | tf_op jit(solution)/shard_map/ppermute | solution.py:53
  101.7 3.0 %collective-permute-start.27 = (bf16[32,5120]{1,0:T(8,128)(2,1)S(1)}, bf16[32,5120]{1,0:T(8,128)(2,1)S(1)}, u32[]{:S(2)}, u32[]{:S(2)}) collective-permute-start(bf16[32,5120]{1,0:T(8,128)(2,1)S(1)} %get-tuple-element.139), channel_id=1, source_target_pairs={{96,0},{25,1},{98,2},{27,3},{100,4},{29,5},{102,6},{31,7},{104,8},... | collective-permute-start | bytes 983048 | tf_op jit(solution)/shard_map/ppermute | solution.py:53
  105.7 7.2 %collective-permute-done.27.g1 = bf16[32,5120]{1,0:T(8,128)(2,1)S(1)} collective-permute-done((bf16[32,5120]{1,0:T(8,128)(2,1)S(1)}, bf16[32,5120]{1,0:T(8,128)(2,1)S(1)}, u32[]{:S(2)}, u32[]{:S(2)}) %collective-permute-start.27) | collective-permute-done | bytes 327712 | tf_op jit(solution)/shard_map/ppermute | solution.py:53
  113.4 3.1 %collective-permute-done.29.g3 = bf16[32,5120]{1,0:T(8,128)(2,1)S(1)} collective-permute-done((bf16[32,5120]{1,0:T(8,128)(2,1)S(1)}, bf16[32,5120]{1,0:T(8,128)(2,1)S(1)}, u32[]{:S(2)}, u32[]{:S(2)}) %collective-permute-start.29) | collective-permute-done | bytes 327712 | tf_op jit(solution)/shard_map/ppermute | solution.py:53
  117.5 2.3 %collective-permute-start.31 = (f32[8,5632]{1,0:T(8,128)S(1)}, f32[8,5632]{1,0:T(8,128)S(1)}, u32[]{:S(2)}, u32[]{:S(2)}) collective-permute-start(f32[8,5632]{1,0:T(8,128)S(1)} %get-tuple-element.144), channel_id=1, source_target_pairs={{16,0},{5,1},{18,2},{7,3},{20,4},{1,5},{22,6},{3,7},{24,8},{13,9},... | collective-permute-start | bytes 540680 | tf_op jit(solution)/shard_map/ppermute | solution.py:53
  122.2 4.0 %collective-permute-done.30.g1 = f32[8,5632]{1,0:T(8,128)S(1)} collective-permute-done((f32[8,5632]{1,0:T(8,128)S(1)}, f32[8,5632]{1,0:T(8,128)S(1)}, u32[]{:S(2)}, u32[]{:S(2)}) %collective-permute-start.30) | collective-permute-done | bytes 180256 | tf_op jit(solution)/shard_map/ppermute | solution.py:53
  127.2 1.8 %collective-permute-start.33 = (f32[8,1024]{1,0:T(8,128)S(1)}, f32[8,1024]{1,0:T(8,128)S(1)}, u32[]{:S(2)}, u32[]{:S(2)}) collective-permute-start(f32[8,1024]{1,0:T(8,128)S(1)} %get-tuple-element.149.refs_0_), channel_id=1, source_target_pairs={{2,0},{33,1},{4,2},{35,3},{6,4},{37,5},{0,6},{39,7},{10,8},{41,9},... | collective-permute-start | bytes 98312 | tf_op jit(solution)/shard_map/ppermute | solution.py:53
  129.0 2.2 %collective-permute-start.34 = (f32[8,1024]{1,0:T(8,128)S(1)}, f32[8,1024]{1,0:T(8,128)S(1)}, u32[]{:S(2)}, u32[]{:S(2)}) collective-permute-start(f32[8,1024]{1,0:T(8,128)S(1)} %get-tuple-element.149.refs_0_), channel_id=1, source_target_pairs={{4,0},{65,1},{6,2},{67,3},{0,4},{69,5},{2,6},{71,7},{12,8},{73,9},... | collective-permute-start | bytes 98312 | tf_op jit(solution)/shard_map/ppermute | solution.py:53
  131.1 2.5 %collective-permute-start.35 = (f32[8,1024]{1,0:T(8,128)S(1)}, f32[8,1024]{1,0:T(8,128)S(1)}, u32[]{:S(2)}, u32[]{:S(2)}) collective-permute-start(f32[8,1024]{1,0:T(8,128)S(1)} %get-tuple-element.149.refs_0_), channel_id=1, source_target_pairs={{6,0},{97,1},{0,2},{99,3},{2,4},{101,5},{4,6},{103,7},{14,8},{105,... | collective-permute-start | bytes 98312 | tf_op jit(solution)/shard_map/ppermute | solution.py:53
  133.7 1.9 %collective-permute-start.36 = (f32[8,128]{1,0:T(8,128)S(1)}, f32[8,128]{1,0:T(8,128)S(1)}, u32[]{:S(2)}, u32[]{:S(2)}) collective-permute-start(f32[8,128]{1,0:T(8,128)S(1)} %get-tuple-element.147), channel_id=1, source_target_pairs={{0,0},{1,16},{2,32},{3,17},{4,64},{5,18},{6,96},{7,19},{8,1},{9,20... | collective-permute-start | bytes 12296 | tf_op jit(solution)/shard_map/ppermute | solution.py:545
  135.6 9.6 %collective-permute-done.36 = f32[8,128]{1,0:T(8,128)S(1)} collective-permute-done((f32[8,128]{1,0:T(8,128)S(1)}, f32[8,128]{1,0:T(8,128)S(1)}, u32[]{:S(2)}, u32[]{:S(2)}) %collective-permute-start.36) | collective-permute-done | bytes 4128 | tf_op jit(solution)/shard_map/ppermute | solution.py:545
  146.6 2.4 %finish.1 = (f32[64,1024]{1,0:T(8,128)}, f32[1,64]{1,0:T(1,128)}, f32[1,128]{1,0:T(1,128)}) custom-call(s32[7]{0:T(128)S(1)} %stack.55.where, f32[4,8,1024]{2,1,0:T(8,128)S(1)} %collect.3.own, f32[4,8,1024]{2,1,0:T(8,128)S(1)} %collective-permute-done.37.oth, s32[1024,64]{1,0:T(8,128)S(1)} %copy.24.labels, f32[1,64]{1,0:T(1,128)S(1)} %bitcast.45, ...), custom_call_target="tpu_custom_call" | custom-call | flops 1000000 | tf_op jit(solution)/shard_map/finish/pallas_call | solution.py:255
  (95 shorter events, 32.2 us)
Async XLA Ops:
  0.6 7.6 %collective-permute-start = (bf16[128,288]{0,1:T(8,128)(2,1)}, bf16[128,288]{0,1:T(8,128)(2,1)S(1)}, u32[]{:S(2)}, u32[]{:S(2)}) collective-permute-start(bf16[128,288]{0,1:T(8,128)(2,1)} %param.9), channel_id=1, source_target_pairs={{8,0},{9,1},{10,2},{11,3},{12,4},{13,5},{14,6},{15,7},{16,8},{17,9... | collective-permute-start | bytes 221192 | tf_op jit(solution)/shard_map/ppermute | solution.py:53
  4.7 6.3 %collective-permute-start.1 = (bf16[128,288]{0,1:T(8,128)(2,1)}, bf16[128,288]{0,1:T(8,128)(2,1)S(1)}, u32[]{:S(2)}, u32[]{:S(2)}) collective-permute-start(bf16[128,288]{0,1:T(8,128)(2,1)} %param.9), channel_id=1, source_target_pairs={{16,0},{17,1},{18,2},{19,3},{20,4},{21,5},{22,6},{23,7},{24,8},{25... | collective-permute-start | bytes 221192 | tf_op jit(solution)/shard_map/ppermute | solution.py:53
  4.7 6.7 %collective-permute-start.2 = (bf16[128,288]{0,1:T(8,128)(2,1)}, bf16[128,288]{0,1:T(8,128)(2,1)S(1)}, u32[]{:S(2)}, u32[]{:S(2)}) collective-permute-start(bf16[128,288]{0,1:T(8,128)(2,1)} %param.9), channel_id=1, source_target_pairs={{24,0},{25,1},{26,2},{27,3},{28,4},{29,5},{30,6},{31,7},{0,8},{1,9... | collective-permute-start | bytes 221192 | tf_op jit(solution)/shard_map/ppermute | solution.py:53
  11.9 11.6 %collective-permute-start.3 = (bf16[128,1152]{1,0:T(8,128)(2,1)S(1)}, bf16[128,1152]{1,0:T(8,128)(2,1)S(1)}, u32[]{:S(2)}, u32[]{:S(2)}) collective-permute-start(bf16[128,1152]{1,0:T(8,128)(2,1)S(1)} %settle.1.refs_0_), channel_id=1, source_target_pairs={{32,0},{3,1},{34,2},{5,3},{36,4},{7,5},{38,6},{1,7},{40,8},{11,9},... | collective-permute-start | bytes 884744 | tf_op jit(solution)/shard_map/ppermute | solution.py:53
  12.7 10.8 %collective-permute-start.4 = (bf16[128,1152]{1,0:T(8,128)(2,1)S(1)}, bf16[128,1152]{1,0:T(8,128)(2,1)S(1)}, u32[]{:S(2)}, u32[]{:S(2)}) collective-permute-start(bf16[128,1152]{1,0:T(8,128)(2,1)S(1)} %settle.1.refs_0_), channel_id=1, source_target_pairs={{64,0},{5,1},{66,2},{7,3},{68,4},{1,5},{70,6},{3,7},{72,8},{13,9},... | collective-permute-start | bytes 884744 | tf_op jit(solution)/shard_map/ppermute | solution.py:53
  13.6 10.3 %collective-permute-start.5 = (bf16[128,1152]{1,0:T(8,128)(2,1)S(1)}, bf16[128,1152]{1,0:T(8,128)(2,1)S(1)}, u32[]{:S(2)}, u32[]{:S(2)}) collective-permute-start(bf16[128,1152]{1,0:T(8,128)(2,1)S(1)} %settle.1.refs_0_), channel_id=1, source_target_pairs={{96,0},{7,1},{98,2},{1,3},{100,4},{3,5},{102,6},{5,7},{104,8},{15,... | collective-permute-start | bytes 884744 | tf_op jit(solution)/shard_map/ppermute | solution.py:53
  24.0 2.9 %collective-permute-start.8 = (bf16[4,128,1152]{2,1,0:T(8,128)(2,1)S(1)}, bf16[4,128,1152]{2,1,0:T(8,128)(2,1)S(1)}, u32[]{:S(2)}, u32[]{:S(2)}) collective-permute-start(bf16[4,128,1152]{2,1,0:T(8,128)(2,1)S(1)} %collect.2.refs_0_.block), channel_id=1, source_target_pairs={{0,1},{1,0},{2,3},{3,2},{4,5},{5,4},{6,7},{7,6},{8,9},{9,8},{10,11... | collective-permute-start | bytes 3538952 | tf_op jit(solution)/shard_map/ppermute | solution.py:58
  24.1 16.3 %collective-permute-start.6 = (bf16[4,128,1152]{2,1,0:T(8,128)(2,1)S(1)}, bf16[4,128,1152]{2,1,0:T(8,128)(2,1)S(1)}, u32[]{:S(2)}, u32[]{:S(2)}) collective-permute-start(bf16[4,128,1152]{2,1,0:T(8,128)(2,1)S(1)} %collect.2.refs_0_.block), channel_id=1, source_target_pairs={{2,0},{33,1},{4,2},{35,3},{6,4},{37,5},{0,6},{39,7},{10,8},{41,9},... | collective-permute-start | bytes 3538952 | tf_op jit(solution)/shard_map/ppermute | solution.py:53
  24.7 16.9 %collective-permute-start.7 = (bf16[4,128,1152]{2,1,0:T(8,128)(2,1)S(1)}, bf16[4,128,1152]{2,1,0:T(8,128)(2,1)S(1)}, u32[]{:S(2)}, u32[]{:S(2)}) collective-permute-start(bf16[4,128,1152]{2,1,0:T(8,128)(2,1)S(1)} %collect.2.refs_0_.block), channel_id=1, source_target_pairs={{6,0},{97,1},{0,2},{99,3},{2,4},{101,5},{4,6},{103,7},{14,8},{105,... | collective-permute-start | bytes 3538952 | tf_op jit(solution)/shard_map/ppermute | solution.py:53
  41.6 4.0 %collective-permute-start.12 = (bf16[4,128,1152]{2,1,0:T(8,128)(2,1)S(1)}, bf16[4,128,1152]{2,1,0:T(8,128)(2,1)S(1)}, u32[]{:S(2)}, u32[]{:S(2)}) collective-permute-start(bf16[4,128,1152]{2,1,0:T(8,128)(2,1)S(1)} %collective-permute-done.6.a.refs_0_.side1), channel_id=1, source_target_pairs={{0,1},{1,0},{2,3},{3,2},{4,5},{5,4},{6,7},{7,6},{8,9},{9,8},{10,11... | collective-permute-start | bytes 3538952 | tf_op jit(solution)/shard_map/ppermute | solution.py:58
  41.6 8.2 %collective-permute-start.11 = (bf16[4,128,1152]{2,1,0:T(8,128)(2,1)S(1)}, bf16[4,128,1152]{2,1,0:T(8,128)(2,1)S(1)}, u32[]{:S(2)}, u32[]{:S(2)}) collective-permute-start(bf16[4,128,1152]{2,1,0:T(8,128)(2,1)S(1)} %collective-permute-done.7.b.refs_0_.side3), channel_id=1, source_target_pairs={{0,1},{1,0},{2,3},{3,2},{4,5},{5,4},{6,7},{7,6},{8,9},{9,8},{10,11... | collective-permute-start | bytes 3538952 | tf_op jit(solution)/shard_map/ppermute | solution.py:58
  42.2 11.8 %collective-permute-start.10 = (bf16[2,128,1152]{2,1,0:T(8,128)(2,1)S(1)}, bf16[2,128,1152]{2,1,0:T(8,128)(2,1)S(1)}, u32[]{:S(2)}, u32[]{:S(2)}) collective-permute-start(bf16[2,128,1152]{2,1,0:T(8,128)(2,1)S(1)} %get-tuple-element.96), channel_id=1, source_target_pairs={{6,0},{97,1},{0,2},{99,3},{2,4},{101,5},{4,6},{103,7},{14,8},{105,... | collective-permute-start | bytes 1769480 | tf_op jit(solution)/shard_map/ppermute | solution.py:53
  43.1 11.0 %collective-permute-start.9 = (bf16[2,128,1152]{2,1,0:T(8,128)(2,1)S(1)}, bf16[2,128,1152]{2,1,0:T(8,128)(2,1)S(1)}, u32[]{:S(2)}, u32[]{:S(2)}) collective-permute-start(bf16[2,128,1152]{2,1,0:T(8,128)(2,1)S(1)} %get-tuple-element.95), channel_id=1, source_target_pairs={{2,0},{33,1},{4,2},{35,3},{6,4},{37,5},{0,6},{39,7},{10,8},{41,9},... | collective-permute-start | bytes 1769480 | tf_op jit(solution)/shard_map/ppermute | solution.py:53
  54.0 2.9 %collective-permute-start.13 = (bf16[2,128,1152]{2,1,0:T(8,128)(2,1)S(1)}, bf16[2,128,1152]{2,1,0:T(8,128)(2,1)S(1)}, u32[]{:S(2)}, u32[]{:S(2)}) collective-permute-start(bf16[2,128,1152]{2,1,0:T(8,128)(2,1)S(1)} %collective-permute-done.9.refs_0_.low), channel_id=1, source_target_pairs={{0,1},{1,0},{2,3},{3,2},{4,5},{5,4},{6,7},{7,6},{8,9},{9,8},{10,11... | collective-permute-start | bytes 1769480 | tf_op jit(solution)/shard_map/ppermute | solution.py:58
  62.9 3.0 %collective-permute-start.16 = (bf16[128,2432]{1,0:T(8,128)(2,1)S(1)}, bf16[128,2432]{1,0:T(8,128)(2,1)S(1)}, u32[]{:S(2)}, u32[]{:S(2)}) collective-permute-start(bf16[128,2432]{1,0:T(8,128)(2,1)S(1)} %get-tuple-element.111), channel_id=1, source_target_pairs={{0,1},{1,0},{2,3},{3,2},{4,5},{5,4},{6,7},{7,6},{8,9},{9,8},{10,11... | collective-permute-start | bytes 1867784 | tf_op jit(solution)/shard_map/ppermute | solution.py:58
  66.4 11.7 %collective-permute-start.17 = (bf16[64,4992]{1,0:T(8,128)(2,1)S(1)}, bf16[64,4992]{1,0:T(8,128)(2,1)S(1)}, u32[]{:S(2)}, u32[]{:S(2)}) collective-permute-start(bf16[64,4992]{1,0:T(8,128)(2,1)S(1)} %get-tuple-element.116), channel_id=1, source_target_pairs={{6,0},{97,1},{0,2},{99,3},{2,4},{101,5},{4,6},{103,7},{14,8},{105,... | collective-permute-start | bytes 1916936 | tf_op jit(solution)/shard_map/ppermute | solution.py:53
  68.3 11.6 %collective-permute-start.18 = (bf16[64,4992]{1,0:T(8,128)(2,1)S(1)}, bf16[64,4992]{1,0:T(8,128)(2,1)S(1)}, u32[]{:S(2)}, u32[]{:S(2)}) collective-permute-start(bf16[64,4992]{1,0:T(8,128)(2,1)S(1)} %get-tuple-element.117), channel_id=1, source_target_pairs={{2,0},{33,1},{4,2},{35,3},{6,4},{37,5},{0,6},{39,7},{10,8},{41,9},... | collective-permute-start | bytes 1916936 | tf_op jit(solution)/shard_map/ppermute | solution.py:53
  73.2 6.8 %collective-permute-start.22 = (bf16[128,2432]{1,0:T(8,128)(2,1)S(1)}, bf16[128,2432]{1,0:T(8,128)(2,1)S(1)}, u32[]{:S(2)}, u32[]{:S(2)}) collective-permute-start(bf16[128,2432]{1,0:T(8,128)(2,1)S(1)} %get-tuple-element.129), channel_id=1, source_target_pairs={{0,1},{1,0},{2,3},{3,2},{4,5},{5,4},{6,7},{7,6},{8,9},{9,8},{10,11... | collective-permute-start | bytes 1867784 | tf_op jit(solution)/shard_map/ppermute | solution.py:58
  77.0 3.9 %collective-permute-start.20 = (bf16[128,2432]{1,0:T(8,128)(2,1)S(1)}, bf16[128,2432]{1,0:T(8,128)(2,1)S(1)}, u32[]{:S(2)}, u32[]{:S(2)}) collective-permute-start(bf16[128,2432]{1,0:T(8,128)(2,1)S(1)} %get-tuple-element.125), channel_id=1, source_target_pairs={{0,1},{1,0},{2,3},{3,2},{4,5},{5,4},{6,7},{7,6},{8,9},{9,8},{10,11... | collective-permute-start | bytes 1867784 | tf_op jit(solution)/shard_map/ppermute | solution.py:58
  81.6 17.8 %collective-permute-start.25 = (bf16[128,4736]{1,0:T(8,128)(2,1)S(1)}, bf16[128,4736]{1,0:T(8,128)(2,1)S(1)}, u32[]{:S(2)}, u32[]{:S(2)}) collective-permute-start(bf16[128,4736]{1,0:T(8,128)(2,1)S(1)} %pair_sum.4), channel_id=1, source_target_pairs={{6,0},{97,1},{0,2},{99,3},{2,4},{101,5},{4,6},{103,7},{14,8},{105,... | collective-permute-start | bytes 3637256 | tf_op jit(solution)/shard_map/ppermute | solution.py:53
  83.4 16.9 %collective-permute-start.26 = (bf16[128,4736]{1,0:T(8,128)(2,1)S(1)}, bf16[128,4736]{1,0:T(8,128)(2,1)S(1)}, u32[]{:S(2)}, u32[]{:S(2)}) collective-permute-start(bf16[128,4736]{1,0:T(8,128)(2,1)S(1)} %pair_sum.5), channel_id=1, source_target_pairs={{2,0},{33,1},{4,2},{35,3},{6,4},{37,5},{0,6},{39,7},{10,8},{41,9},... | collective-permute-start | bytes 3637256 | tf_op jit(solution)/shard_map/ppermute | solution.py:53
  89.3 3.0 %collective-permute-start.24 = (bf16[128,2432]{1,0:T(8,128)(2,1)S(1)}, bf16[128,2432]{1,0:T(8,128)(2,1)S(1)}, u32[]{:S(2)}, u32[]{:S(2)}) collective-permute-start(bf16[128,2432]{1,0:T(8,128)(2,1)S(1)} %get-tuple-element.135), channel_id=1, source_target_pairs={{0,1},{1,0},{2,3},{3,2},{4,5},{5,4},{6,7},{7,6},{8,9},{9,8},{10,11... | collective-permute-start | bytes 1867784 | tf_op jit(solution)/shard_map/ppermute | solution.py:58
  101.7 11.1 %collective-permute-start.27 = (bf16[32,5120]{1,0:T(8,128)(2,1)S(1)}, bf16[32,5120]{1,0:T(8,128)(2,1)S(1)}, u32[]{:S(2)}, u32[]{:S(2)}) collective-permute-start(bf16[32,5120]{1,0:T(8,128)(2,1)S(1)} %get-tuple-element.139), channel_id=1, source_target_pairs={{96,0},{25,1},{98,2},{27,3},{100,4},{29,5},{102,6},{31,7},{104,8},... | collective-permute-start | bytes 983048 | tf_op jit(solution)/shard_map/ppermute | solution.py:53
  104.7 8.7 %collective-permute-start.28 = (bf16[32,5120]{1,0:T(8,128)(2,1)S(1)}, bf16[32,5120]{1,0:T(8,128)(2,1)S(1)}, u32[]{:S(2)}, u32[]{:S(2)}) collective-permute-start(bf16[32,5120]{1,0:T(8,128)(2,1)S(1)} %get-tuple-element.140), channel_id=1, source_target_pairs={{64,0},{17,1},{66,2},{19,3},{68,4},{21,5},{70,6},{23,7},{72,8},{25... | collective-permute-start | bytes 983048 | tf_op jit(solution)/shard_map/ppermute | solution.py:53
  104.7 11.8 %collective-permute-start.29 = (bf16[32,5120]{1,0:T(8,128)(2,1)S(1)}, bf16[32,5120]{1,0:T(8,128)(2,1)S(1)}, u32[]{:S(2)}, u32[]{:S(2)}) collective-permute-start(bf16[32,5120]{1,0:T(8,128)(2,1)S(1)} %get-tuple-element.141), channel_id=1, source_target_pairs={{32,0},{9,1},{34,2},{11,3},{36,4},{13,5},{38,6},{15,7},{40,8},{17,... | collective-permute-start | bytes 983048 | tf_op jit(solution)/shard_map/ppermute | solution.py:53
  117.4 8.7 %collective-permute-start.30 = (f32[8,5632]{1,0:T(8,128)S(1)}, f32[8,5632]{1,0:T(8,128)S(1)}, u32[]{:S(2)}, u32[]{:S(2)}) collective-permute-start(f32[8,5632]{1,0:T(8,128)S(1)} %get-tuple-element.143), channel_id=1, source_target_pairs={{24,0},{7,1},{26,2},{1,3},{28,4},{3,5},{30,6},{5,7},{0,8},{15,9},{... | collective-permute-start | bytes 540680 | tf_op jit(solution)/shard_map/ppermute | solution.py:53
  117.5 8.6 %collective-permute-start.31 = (f32[8,5632]{1,0:T(8,128)S(1)}, f32[8,5632]{1,0:T(8,128)S(1)}, u32[]{:S(2)}, u32[]{:S(2)}) collective-permute-start(f32[8,5632]{1,0:T(8,128)S(1)} %get-tuple-element.144), channel_id=1, source_target_pairs={{16,0},{5,1},{18,2},{7,3},{20,4},{1,5},{22,6},{3,7},{24,8},{13,9},... | collective-permute-start | bytes 540680 | tf_op jit(solution)/shard_map/ppermute | solution.py:53
  119.8 7.2 %collective-permute-start.32 = (f32[8,5632]{1,0:T(8,128)S(1)}, f32[8,5632]{1,0:T(8,128)S(1)}, u32[]{:S(2)}, u32[]{:S(2)}) collective-permute-start(f32[8,5632]{1,0:T(8,128)S(1)} %get-tuple-element.145), channel_id=1, source_target_pairs={{8,0},{3,1},{10,2},{5,3},{12,4},{7,5},{14,6},{1,7},{16,8},{11,9},{... | collective-permute-start | bytes 540680 | tf_op jit(solution)/shard_map/ppermute | solution.py:53
  127.2 18.0 %collective-permute-start.33 = (f32[8,1024]{1,0:T(8,128)S(1)}, f32[8,1024]{1,0:T(8,128)S(1)}, u32[]{:S(2)}, u32[]{:S(2)}) collective-permute-start(f32[8,1024]{1,0:T(8,128)S(1)} %get-tuple-element.149.refs_0_), channel_id=1, source_target_pairs={{2,0},{33,1},{4,2},{35,3},{6,4},{37,5},{0,6},{39,7},{10,8},{41,9},... | collective-permute-start | bytes 98312 | tf_op jit(solution)/shard_map/ppermute | solution.py:53
  129.0 16.2 %collective-permute-start.34 = (f32[8,1024]{1,0:T(8,128)S(1)}, f32[8,1024]{1,0:T(8,128)S(1)}, u32[]{:S(2)}, u32[]{:S(2)}) collective-permute-start(f32[8,1024]{1,0:T(8,128)S(1)} %get-tuple-element.149.refs_0_), channel_id=1, source_target_pairs={{4,0},{65,1},{6,2},{67,3},{0,4},{69,5},{2,6},{71,7},{12,8},{73,9},... | collective-permute-start | bytes 98312 | tf_op jit(solution)/shard_map/ppermute | solution.py:53
  131.1 14.1 %collective-permute-start.35 = (f32[8,1024]{1,0:T(8,128)S(1)}, f32[8,1024]{1,0:T(8,128)S(1)}, u32[]{:S(2)}, u32[]{:S(2)}) collective-permute-start(f32[8,1024]{1,0:T(8,128)S(1)} %get-tuple-element.149.refs_0_), channel_id=1, source_target_pairs={{6,0},{97,1},{0,2},{99,3},{2,4},{101,5},{4,6},{103,7},{14,8},{105,... | collective-permute-start | bytes 98312 | tf_op jit(solution)/shard_map/ppermute | solution.py:53
  133.7 11.5 %collective-permute-start.36 = (f32[8,128]{1,0:T(8,128)S(1)}, f32[8,128]{1,0:T(8,128)S(1)}, u32[]{:S(2)}, u32[]{:S(2)}) collective-permute-start(f32[8,128]{1,0:T(8,128)S(1)} %get-tuple-element.147), channel_id=1, source_target_pairs={{0,0},{1,16},{2,32},{3,17},{4,64},{5,18},{6,96},{7,19},{8,1},{9,20... | collective-permute-start | bytes 12296 | tf_op jit(solution)/shard_map/ppermute | solution.py:545
  (12 other events, 99.9 us)

commit v2 on v1

--- a/solution.py
+++ b/solution.py
@@ -542,18 +542,17 @@
         owners.append((place(p, c), s[0] * 32 + c * 16 + s[1] * 4 + s[2]))
 
     pulled = [pull(packed, "x", "y", d) for d in (1, 2, 3)]
-    err = lax.ppermute(err, AXES, owners)
-    pulled, packed, err = lax.optimization_barrier((pulled, packed, err))
     mine = collect([packed, *pulled])
     theirs = swap(mine)
-    error = err[:, 0]
+    err = lax.ppermute(err, AXES, owners)
     probe_grad, bias_grad, mean_loss = small_call(
         functools.partial(finish_kernel, 8), "finish",
         [((64, lat), F32), ((1, 64), F32), ((1, 128), F32)],
         where, mine, theirs, labels, probe_bias[None], xa[0], xa[1], xa[2], xa[3], ya,
         scratch=[pltpu.VMEM((8, 128, 128), F32), pltpu.VMEM((8, 128, 128), BF16)],
     )
-    return (error, probe_grad.T, bias_grad[0], mean_loss[0, 0])
+    err, mean_loss = lax.optimization_barrier((err, mean_loss))
+    return (err[:, 0], probe_grad.T, bias_grad[0], mean_loss[0, 0])
 
 
 def solution(mesh):

time: 150 us -> 148 us (0.987)
  waiting for transfers between devices: 56.3 us -> 52.5 us
  starting transfers between devices: 41.3 us -> 43.6 us
    ppermute x1, waiting for transfers between devices: 9.59 us -> 4.72 us  [on_device(): err = lax.ppermute(err, AXES, owners)]
    ppermute x1, starting transfers between devices: 1.91 us -> 4.16 us  [on_device(): err = lax.ppermute(err, AXES, owners)]
    ppermute x23, waiting for transfers between devices: 40.2 us -> 41.8 us  [pull(): return lax.ppermute(value, AXES, pull_perm(axis0, axis1, step))]
  transfers between devices with their start and end apart: 38 -> 38, of which waited for: 22 -> 23; matrix products, arithmetic and copies ran while one was open for 2% -> 2% of each run, Pallas kernels for 23% -> 25%
where the time goes in v2:
time: 148 us
  waiting for transfers between devices  52.5 us (35%)
  Pallas kernels  46.9 us (32%)
  starting transfers between devices  43.6 us (29%)
  local copies, waits for them, and re-layouts  3.29 us (2%)
    ppermute x23, waiting for transfers between devices, pull(): return lax.ppermute(value, AXES, pull_perm(axis0, axis1, step))  41.8 us
    ppermute x23, starting transfers between devices, pull(): return lax.ppermute(value, AXES, pull_perm(axis0, axis1, step))  36 us
    pallas_call x5, Pallas kernels, encode(): pl.pallas_call(functools.partial(encode_kernel, stage, which, 256), in_sp...  17.2 us
    pallas_call x4, Pallas kernels, decode(): pl.pallas_call(functools.partial(decode_kernel, step, 768), in_specs=[pl....  14.6 us
    pallas_call x2, Pallas kernels, load(): pl.pallas_call(load_kernel, in_specs=[pl.BlockSpec(memory_space=pltpu.HBM...  7.6 us
    pallas_call x12, Pallas kernels, small_call(): pl.pallas_call(kernel, in_specs=[smem] * scalars + [vmem] * (len(args) -...  7.56 us
    ppermute x14, waiting for transfers between devices, swap(): return lax.ppermute(value, AXES, pairs)  5.96 us
    ppermute x1, waiting for transfers between devices, on_device(): err = lax.ppermute(err, AXES, owners)  4.72 us
  transfers between devices with their start and end apart: 38, of which 23 were waited for; matrix products, arithmetic and copies ran while one was open for 2% of the time, Pallas kernels for 25%

profile of v2, /device:TPU:26, one launch (start us, length us, event | category | flops | bytes accessed | tf_op | source)
XLA Modules:
  0.0 147.5 jit_solution(5286785656993728152)
XLA Ops:
  0.6 4.1 %collective-permute-start = (bf16[128,288]{0,1:T(8,128)(2,1)}, bf16[128,288]{0,1:T(8,128)(2,1)S(1)}, u32[]{:S(2)}, u32[]{:S(2)}) collective-permute-start(bf16[128,288]{0,1:T(8,128)(2,1)} %param.9), channel_id=1, source_target_pairs={{8,0},{9,1},{10,2},{11,3},{12,4},{13,5},{14,6},{15,7},{16,8},{17,9... | collective-permute-start | bytes 221192 | tf_op jit(solution)/shard_map/ppermute | solution.py:53
  8.3 2.7 %collective-permute-done.1 = bf16[128,288]{0,1:T(8,128)(2,1)S(1)} collective-permute-done((bf16[128,288]{0,1:T(8,128)(2,1)}, bf16[128,288]{0,1:T(8,128)(2,1)S(1)}, u32[]{:S(2)}, u32[]{:S(2)}) %collective-permute-start.1) | collective-permute-done | bytes 73760 | tf_op jit(solution)/shard_map/ppermute | solution.py:53
  13.6 2.2 %collective-permute-start.5 = (bf16[128,1152]{1,0:T(8,128)(2,1)S(1)}, bf16[128,1152]{1,0:T(8,128)(2,1)S(1)}, u32[]{:S(2)}, u32[]{:S(2)}) collective-permute-start(bf16[128,1152]{1,0:T(8,128)(2,1)S(1)} %settle.1.refs_0_), channel_id=1, source_target_pairs={{96,0},{7,1},{98,2},{1,3},{100,4},{3,5},{102,6},{5,7},{104,8},{15,... | collective-permute-start | bytes 884744 | tf_op jit(solution)/shard_map/ppermute | solution.py:53
  15.8 3.8 %load.2.refs_2_ = bf16[4608,1024]{1,0:T(8,128)(2,1)S(1)} custom-call(bf16[4608,1024]{1,0:T(8,128)(2,1)} %source), custom_call_target="tpu_custom_call" | custom-call | flops 1000000 | tf_op jit(solution)/shard_map/load/pallas_call | solution.py:80
  19.6 3.8 %load.3.dec = bf16[1024,4608]{1,0:T(8,128)(2,1)S(1)} custom-call(bf16[1024,4608]{1,0:T(8,128)(2,1)} %source.1), custom_call_target="tpu_custom_call" | custom-call | flops 1000000 | tf_op jit(solution)/shard_map/load/pallas_call | solution.py:80
  26.9 4.1 %encode.5 = (bf16[128,1024]{1,0:T(8,128)(2,1)S(1)}, f32[512,1024]{1,0:T(8,128)S(1)}) custom-call(s32[7]{0:T(128)S(1)} %stack.55.where, bf16[4,128,1152]{2,1,0:T(8,128)(2,1)S(1)} %collect.2.refs_0_.block, bf16[4,128,1152]{2,1,0:T(8,128)(2,1)S(1)} %collective-permute-done.8.refs_1_, bf16[4608,1024]{1,0:T(8,128)(2,1)S(1)} %load.2.refs_2_, ...), custom_call_target="tpu_custom_call" | custom-call | flops 1000000 | tf_op jit(solution)/shard_map/encode/pallas_call | solution.py:184
  31.1 9.3 %collective-permute-done.6.a.refs_0_.side1 = bf16[4,128,1152]{2,1,0:T(8,128)(2,1)S(1)} collective-permute-done((bf16[4,128,1152]{2,1,0:T(8,128)(2,1)S(1)}, bf16[4,128,1152]{2,1,0:T(8,128)(2,1)S(1)}, u32[]{:S(2)}, u32[]{:S(2)}) %collective-permute-start.6) | collective-permute-done | bytes 1179680 | tf_op jit(solution)/shard_map/ppermute | solution.py:53
  43.1 2.6 %collective-permute-start.9 = (bf16[2,128,1152]{2,1,0:T(8,128)(2,1)S(1)}, bf16[2,128,1152]{2,1,0:T(8,128)(2,1)S(1)}, u32[]{:S(2)}, u32[]{:S(2)}) collective-permute-start(bf16[2,128,1152]{2,1,0:T(8,128)(2,1)S(1)} %get-tuple-element.92), channel_id=1, source_target_pairs={{2,0},{33,1},{4,2},{35,3},{6,4},{37,5},{0,6},{39,7},{10,8},{41,9},... | collective-permute-start | bytes 1769480 | tf_op jit(solution)/shard_map/ppermute | solution.py:53
  45.6 4.2 %encode.6 = (bf16[128,1024]{1,0:T(8,128)(2,1)S(1)}, f32[512,1024]{1,0:T(8,128)S(1)}) custom-call(s32[7]{0:T(128)S(1)} %stack.55.where, bf16[4,128,1152]{2,1,0:T(8,128)(2,1)S(1)} %collective-permute-done.6.a.refs_0_.side1, bf16[4,128,1152]{2,1,0:T(8,128)(2,1)S(1)} %collective-permute-done.12.refs_1_, ...), custom_call_target="tpu_custom_call", output_to_operand_aliasing={{1}: (6, {})} | custom-call | flops 1000000 | tf_op jit(solution)/shard_map/encode/pallas_call | solution.py:184
  49.8 4.2 %encode.7 = (bf16[128,1024]{1,0:T(8,128)(2,1)S(1)}, f32[512,1024]{1,0:T(8,128)S(1)}) custom-call(s32[7]{0:T(128)S(1)} %stack.55.where, bf16[4,128,1152]{2,1,0:T(8,128)(2,1)S(1)} %collective-permute-done.7.b.refs_0_.side3, bf16[4,128,1152]{2,1,0:T(8,128)(2,1)S(1)} %collective-permute-done.11.refs_1_, ...), custom_call_target="tpu_custom_call", output_to_operand_aliasing={{1}: (6, {})} | custom-call | flops 1000000 | tf_op jit(solution)/shard_map/encode/pallas_call | solution.py:184
  54.6 2.3 %encode.8 = (bf16[128,1024]{1,0:T(8,128)(2,1)S(1)}, bf16[512,1024]{1,0:T(8,128)(2,1)S(1)}) custom-call(s32[7]{0:T(128)S(1)} %stack.55.where, bf16[2,128,1152]{2,1,0:T(8,128)(2,1)S(1)} %collective-permute-done.9.refs_0_.low, bf16[2,128,1152]{2,1,0:T(8,128)(2,1)S(1)} %collective-permute-done.10.refs_1_.high, bf16[4608,1024]{1,0:T(8,128)(2,1)S(1)} %load.2.refs_2_, ...), custom_call_target="tpu_custom_call" | custom-call | flops 1000000 | tf_op jit(solution)/shard_map/encode/pallas_call | solution.py:184
  57.1 2.4 %encode.9 = (bf16[128,1024]{1,0:T(8,128)(2,1)S(1)}, bf16[512,1024]{1,0:T(8,128)(2,1)S(1)}) custom-call(s32[7]{0:T(128)S(1)} %stack.55.where, bf16[2,128,1152]{2,1,0:T(8,128)(2,1)S(1)} %collective-permute-done.13.refs_0_, bf16[2,128,1152]{2,1,0:T(8,128)(2,1)S(1)} %collective-permute-done.14.refs_1_, ...), custom_call_target="tpu_custom_call", output_to_operand_aliasing={{0}: (7, {}), {1}: (8, {})} | custom-call | flops 1000000 | tf_op jit(solution)/shard_map/encode/pallas_call | solution.py:184
  59.5 3.4 %decode.4 = (bf16[128,4736]{1,0:T(8,128)(2,1)S(1)}, bf16[128,2304]{1,0:T(8,128)(2,1)S(1)}, bf16[128,2432]{1,0:T(8,128)(2,1)S(1)}) custom-call(s32[7]{0:T(128)S(1)} %stack.55.where, bf16[128,1024]{1,0:T(8,128)(2,1)S(1)} %get-tuple-element.102.xa.refs_2_, bf16[4,128,1024]{2,1,0:T(8,128)(2,1)S(1)} %bitcast.30, bf16[1024,4608]{1,0:T(8,128)(2,1)S(1)} %load.3.dec, ...), custom_call_target="tpu_custom_call" | custom-call | flops 1000000 | tf_op jit(solution)/shard_map/decode/pallas_call | solution.py:240
  63.5 2.4 %collective-permute-done.15.b0 = bf16[128,2304]{1,0:T(8,128)(2,1)S(1)} collective-permute-done((bf16[128,2304]{1,0:T(8,128)(2,1)S(1)}, bf16[128,2304]{1,0:T(8,128)(2,1)S(1)}, u32[]{:S(2)}, u32[]{:S(2)}) %collective-permute-start.15) | collective-permute-done | bytes 589856 | tf_op jit(solution)/shard_map/ppermute | solution.py:58
  66.4 1.9 %collective-permute-start.17 = (bf16[64,4992]{1,0:T(8,128)(2,1)S(1)}, bf16[64,4992]{1,0:T(8,128)(2,1)S(1)}, u32[]{:S(2)}, u32[]{:S(2)}) collective-permute-start(bf16[64,4992]{1,0:T(8,128)(2,1)S(1)} %get-tuple-element.113), channel_id=1, source_target_pairs={{6,0},{97,1},{0,2},{99,3},{2,4},{101,5},{4,6},{103,7},{14,8},{105,... | collective-permute-start | bytes 1916936 | tf_op jit(solution)/shard_map/ppermute | solution.py:53
  69.8 3.4 %decode.6 = (bf16[128,4736]{1,0:T(8,128)(2,1)S(1)}, bf16[128,2304]{1,0:T(8,128)(2,1)S(1)}, bf16[128,2432]{1,0:T(8,128)(2,1)S(1)}) custom-call(s32[7]{0:T(128)S(1)} %stack.55.where, bf16[128,1024]{1,0:T(8,128)(2,1)S(1)} %get-tuple-element.117.xa.refs_3_, bf16[4,128,1024]{2,1,0:T(8,128)(2,1)S(1)} %bitcast.31, bf16[1024,4608]{1,0:T(8,128)(2,1)S(1)} %load.3.dec, ...), custom_call_target="tpu_custom_call" | custom-call | flops 1000000 | tf_op jit(solution)/shard_map/decode/pallas_call | solution.py:240
  73.5 3.4 %decode.5 = (bf16[128,4736]{1,0:T(8,128)(2,1)S(1)}, bf16[128,2304]{1,0:T(8,128)(2,1)S(1)}, bf16[128,2432]{1,0:T(8,128)(2,1)S(1)}) custom-call(s32[7]{0:T(128)S(1)} %stack.55.where, bf16[128,1024]{1,0:T(8,128)(2,1)S(1)} %get-tuple-element.115.xa.refs_1_, bf16[4,128,1024]{2,1,0:T(8,128)(2,1)S(1)} %bitcast.32, bf16[1024,4608]{1,0:T(8,128)(2,1)S(1)} %load.3.dec, ...), custom_call_target="tpu_custom_call" | custom-call | flops 1000000 | tf_op jit(solution)/shard_map/decode/pallas_call | solution.py:240
  81.6 1.8 %collective-permute-start.25 = (bf16[128,4736]{1,0:T(8,128)(2,1)S(1)}, bf16[128,4736]{1,0:T(8,128)(2,1)S(1)}, u32[]{:S(2)}, u32[]{:S(2)}) collective-permute-start(bf16[128,4736]{1,0:T(8,128)(2,1)S(1)} %pair_sum.4), channel_id=1, source_target_pairs={{6,0},{97,1},{0,2},{99,3},{2,4},{101,5},{4,6},{103,7},{14,8},{105,... | collective-permute-start | bytes 3637256 | tf_op jit(solution)/shard_map/ppermute | solution.py:53
  84.9 4.4 %decode.7 = (bf16[128,4736]{1,0:T(8,128)(2,1)S(1)}, bf16[128,2304]{1,0:T(8,128)(2,1)S(1)}, bf16[128,2432]{1,0:T(8,128)(2,1)S(1)}) custom-call(s32[7]{0:T(128)S(1)} %stack.55.where, bf16[128,1024]{1,0:T(8,128)(2,1)S(1)} %get-tuple-element.129.xa.refs_0_, bf16[4,128,1024]{2,1,0:T(8,128)(2,1)S(1)} %bitcast.33, bf16[1024,4608]{1,0:T(8,128)(2,1)S(1)} %load.3.dec, ...), custom_call_target="tpu_custom_call" | custom-call | flops 1000000 | tf_op jit(solution)/shard_map/decode/pallas_call | solution.py:240
  89.9 2.4 %collective-permute-done.23.b0 = bf16[128,2304]{1,0:T(8,128)(2,1)S(1)} collective-permute-done((bf16[128,2304]{1,0:T(8,128)(2,1)S(1)}, bf16[128,2304]{1,0:T(8,128)(2,1)S(1)}, u32[]{:S(2)}, u32[]{:S(2)}) %collective-permute-start.23) | collective-permute-done | bytes 589856 | tf_op jit(solution)/shard_map/ppermute | solution.py:58
  92.3 7.1 %collective-permute-done.25.g1 = bf16[128,4736]{1,0:T(8,128)(2,1)S(1)} collective-permute-done((bf16[128,4736]{1,0:T(8,128)(2,1)S(1)}, bf16[128,4736]{1,0:T(8,128)(2,1)S(1)}, u32[]{:S(2)}, u32[]{:S(2)}) %collective-permute-start.25) | collective-permute-done | bytes 1212448 | tf_op jit(solution)/shard_map/ppermute | solution.py:53
  101.7 3.0 %collective-permute-start.27 = (bf16[32,5120]{1,0:T(8,128)(2,1)S(1)}, bf16[32,5120]{1,0:T(8,128)(2,1)S(1)}, u32[]{:S(2)}, u32[]{:S(2)}) collective-permute-start(bf16[32,5120]{1,0:T(8,128)(2,1)S(1)} %get-tuple-element.136), channel_id=1, source_target_pairs={{96,0},{25,1},{98,2},{27,3},{100,4},{29,5},{102,6},{31,7},{104,8},... | collective-permute-start | bytes 983048 | tf_op jit(solution)/shard_map/ppermute | solution.py:53
  105.7 7.2 %collective-permute-done.27.g1 = bf16[32,5120]{1,0:T(8,128)(2,1)S(1)} collective-permute-done((bf16[32,5120]{1,0:T(8,128)(2,1)S(1)}, bf16[32,5120]{1,0:T(8,128)(2,1)S(1)}, u32[]{:S(2)}, u32[]{:S(2)}) %collective-permute-start.27) | collective-permute-done | bytes 327712 | tf_op jit(solution)/shard_map/ppermute | solution.py:53
  113.4 3.1 %collective-permute-done.29.g3 = bf16[32,5120]{1,0:T(8,128)(2,1)S(1)} collective-permute-done((bf16[32,5120]{1,0:T(8,128)(2,1)S(1)}, bf16[32,5120]{1,0:T(8,128)(2,1)S(1)}, u32[]{:S(2)}, u32[]{:S(2)}) %collective-permute-start.29) | collective-permute-done | bytes 327712 | tf_op jit(solution)/shard_map/ppermute | solution.py:53
  117.5 2.3 %collective-permute-start.31 = (f32[8,5632]{1,0:T(8,128)S(1)}, f32[8,5632]{1,0:T(8,128)S(1)}, u32[]{:S(2)}, u32[]{:S(2)}) collective-permute-start(f32[8,5632]{1,0:T(8,128)S(1)} %get-tuple-element.141), channel_id=1, source_target_pairs={{16,0},{5,1},{18,2},{7,3},{20,4},{1,5},{22,6},{3,7},{24,8},{13,9},... | collective-permute-start | bytes 540680 | tf_op jit(solution)/shard_map/ppermute | solution.py:53
  122.2 4.0 %collective-permute-done.30.g1 = f32[8,5632]{1,0:T(8,128)S(1)} collective-permute-done((f32[8,5632]{1,0:T(8,128)S(1)}, f32[8,5632]{1,0:T(8,128)S(1)}, u32[]{:S(2)}, u32[]{:S(2)}) %collective-permute-start.30) | collective-permute-done | bytes 180256 | tf_op jit(solution)/shard_map/ppermute | solution.py:53
  127.2 1.8 %collective-permute-start.34 = (f32[8,1024]{1,0:T(8,128)S(1)}, f32[8,1024]{1,0:T(8,128)S(1)}, u32[]{:S(2)}, u32[]{:S(2)}) collective-permute-start(f32[8,1024]{1,0:T(8,128)S(1)} %get-tuple-element.144.refs_0_), channel_id=1, source_target_pairs={{2,0},{33,1},{4,2},{35,3},{6,4},{37,5},{0,6},{39,7},{10,8},{41,9},... | collective-permute-start | bytes 98312 | tf_op jit(solution)/shard_map/ppermute | solution.py:53
  129.0 2.2 %collective-permute-start.35 = (f32[8,1024]{1,0:T(8,128)S(1)}, f32[8,1024]{1,0:T(8,128)S(1)}, u32[]{:S(2)}, u32[]{:S(2)}) collective-permute-start(f32[8,1024]{1,0:T(8,128)S(1)} %get-tuple-element.144.refs_0_), channel_id=1, source_target_pairs={{4,0},{65,1},{6,2},{67,3},{0,4},{69,5},{2,6},{71,7},{12,8},{73,9},... | collective-permute-start | bytes 98312 | tf_op jit(solution)/shard_map/ppermute | solution.py:53
  131.1 2.5 %collective-permute-start.36 = (f32[8,1024]{1,0:T(8,128)S(1)}, f32[8,1024]{1,0:T(8,128)S(1)}, u32[]{:S(2)}, u32[]{:S(2)}) collective-permute-start(f32[8,1024]{1,0:T(8,128)S(1)} %get-tuple-element.144.refs_0_), channel_id=1, source_target_pairs={{6,0},{97,1},{0,2},{99,3},{2,4},{101,5},{4,6},{103,7},{14,8},{105,... | collective-permute-start | bytes 98312 | tf_op jit(solution)/shard_map/ppermute | solution.py:53
  135.4 4.2 %collective-permute-start.33 = (f32[8,128]{1,0:T(8,128)S(1)}, f32[8,128]{1,0:T(8,128)S(1)}, u32[]{:S(2)}, u32[]{:S(2)}) collective-permute-start(f32[8,128]{1,0:T(8,128)S(1)} %get-tuple-element.143), channel_id=1, source_target_pairs={{0,0},{1,16},{2,32},{3,17},{4,64},{5,18},{6,96},{7,19},{8,1},{9,20... | collective-permute-start | bytes 12296 | tf_op jit(solution)/shard_map/ppermute | solution.py:547
  139.8 2.4 %finish.1 = (f32[64,1024]{1,0:T(8,128)}, f32[1,64]{1,0:T(1,128)}, f32[1,128]{1,0:T(1,128)}) custom-call(s32[7]{0:T(128)S(1)} %stack.55.where, f32[4,8,1024]{2,1,0:T(8,128)S(1)} %collect.3.own, f32[4,8,1024]{2,1,0:T(8,128)S(1)} %collective-permute-done.37.oth, s32[1024,64]{1,0:T(8,128)S(1)} %copy.24.labels, f32[1,64]{1,0:T(1,128)S(1)} %bitcast.45, ...), custom_call_target="tpu_custom_call" | custom-call | flops 1000000 | tf_op jit(solution)/shard_map/finish/pallas_call | solution.py:255
  142.2 4.7 %collective-permute-done.33 = f32[8,128]{1,0:T(8,128)S(1)} collective-permute-done((f32[8,128]{1,0:T(8,128)S(1)}, f32[8,128]{1,0:T(8,128)S(1)}, u32[]{:S(2)}, u32[]{:S(2)}) %collective-permute-start.33) | collective-permute-done | bytes 4128 | tf_op jit(solution)/shard_map/ppermute | solution.py:547
  (95 shorter events, 33.2 us)
Async XLA Ops:
  0.6 7.6 %collective-permute-start = (bf16[128,288]{0,1:T(8,128)(2,1)}, bf16[128,288]{0,1:T(8,128)(2,1)S(1)}, u32[]{:S(2)}, u32[]{:S(2)}) collective-permute-start(bf16[128,288]{0,1:T(8,128)(2,1)} %param.9), channel_id=1, source_target_pairs={{8,0},{9,1},{10,2},{11,3},{12,4},{13,5},{14,6},{15,7},{16,8},{17,9... | collective-permute-start | bytes 221192 | tf_op jit(solution)/shard_map/ppermute | solution.py:53
  4.7 6.3 %collective-permute-start.1 = (bf16[128,288]{0,1:T(8,128)(2,1)}, bf16[128,288]{0,1:T(8,128)(2,1)S(1)}, u32[]{:S(2)}, u32[]{:S(2)}) collective-permute-start(bf16[128,288]{0,1:T(8,128)(2,1)} %param.9), channel_id=1, source_target_pairs={{16,0},{17,1},{18,2},{19,3},{20,4},{21,5},{22,6},{23,7},{24,8},{25... | collective-permute-start | bytes 221192 | tf_op jit(solution)/shard_map/ppermute | solution.py:53
  4.7 6.7 %collective-permute-start.2 = (bf16[128,288]{0,1:T(8,128)(2,1)}, bf16[128,288]{0,1:T(8,128)(2,1)S(1)}, u32[]{:S(2)}, u32[]{:S(2)}) collective-permute-start(bf16[128,288]{0,1:T(8,128)(2,1)} %param.9), channel_id=1, source_target_pairs={{24,0},{25,1},{26,2},{27,3},{28,4},{29,5},{30,6},{31,7},{0,8},{1,9... | collective-permute-start | bytes 221192 | tf_op jit(solution)/shard_map/ppermute | solution.py:53
  11.9 11.6 %collective-permute-start.3 = (bf16[128,1152]{1,0:T(8,128)(2,1)S(1)}, bf16[128,1152]{1,0:T(8,128)(2,1)S(1)}, u32[]{:S(2)}, u32[]{:S(2)}) collective-permute-start(bf16[128,1152]{1,0:T(8,128)(2,1)S(1)} %settle.1.refs_0_), channel_id=1, source_target_pairs={{32,0},{3,1},{34,2},{5,3},{36,4},{7,5},{38,6},{1,7},{40,8},{11,9},... | collective-permute-start | bytes 884744 | tf_op jit(solution)/shard_map/ppermute | solution.py:53
  12.7 10.8 %collective-permute-start.4 = (bf16[128,1152]{1,0:T(8,128)(2,1)S(1)}, bf16[128,1152]{1,0:T(8,128)(2,1)S(1)}, u32[]{:S(2)}, u32[]{:S(2)}) collective-permute-start(bf16[128,1152]{1,0:T(8,128)(2,1)S(1)} %settle.1.refs_0_), channel_id=1, source_target_pairs={{64,0},{5,1},{66,2},{7,3},{68,4},{1,5},{70,6},{3,7},{72,8},{13,9},... | collective-permute-start | bytes 884744 | tf_op jit(solution)/shard_map/ppermute | solution.py:53
  13.6 10.3 %collective-permute-start.5 = (bf16[128,1152]{1,0:T(8,128)(2,1)S(1)}, bf16[128,1152]{1,0:T(8,128)(2,1)S(1)}, u32[]{:S(2)}, u32[]{:S(2)}) collective-permute-start(bf16[128,1152]{1,0:T(8,128)(2,1)S(1)} %settle.1.refs_0_), channel_id=1, source_target_pairs={{96,0},{7,1},{98,2},{1,3},{100,4},{3,5},{102,6},{5,7},{104,8},{15,... | collective-permute-start | bytes 884744 | tf_op jit(solution)/shard_map/ppermute | solution.py:53
  24.1 16.3 %collective-permute-start.6 = (bf16[4,128,1152]{2,1,0:T(8,128)(2,1)S(1)}, bf16[4,128,1152]{2,1,0:T(8,128)(2,1)S(1)}, u32[]{:S(2)}, u32[]{:S(2)}) collective-permute-start(bf16[4,128,1152]{2,1,0:T(8,128)(2,1)S(1)} %collect.2.refs_0_.block), channel_id=1, source_target_pairs={{2,0},{33,1},{4,2},{35,3},{6,4},{37,5},{0,6},{39,7},{10,8},{41,9},... | collective-permute-start | bytes 3538952 | tf_op jit(solution)/shard_map/ppermute | solution.py:53
  24.7 16.9 %collective-permute-start.7 = (bf16[4,128,1152]{2,1,0:T(8,128)(2,1)S(1)}, bf16[4,128,1152]{2,1,0:T(8,128)(2,1)S(1)}, u32[]{:S(2)}, u32[]{:S(2)}) collective-permute-start(bf16[4,128,1152]{2,1,0:T(8,128)(2,1)S(1)} %collect.2.refs_0_.block), channel_id=1, source_target_pairs={{6,0},{97,1},{0,2},{99,3},{2,4},{101,5},{4,6},{103,7},{14,8},{105,... | collective-permute-start | bytes 3538952 | tf_op jit(solution)/shard_map/ppermute | solution.py:53
  41.6 4.0 %collective-permute-start.12 = (bf16[4,128,1152]{2,1,0:T(8,128)(2,1)S(1)}, bf16[4,128,1152]{2,1,0:T(8,128)(2,1)S(1)}, u32[]{:S(2)}, u32[]{:S(2)}) collective-permute-start(bf16[4,128,1152]{2,1,0:T(8,128)(2,1)S(1)} %collective-permute-done.6.a.refs_0_.side1), channel_id=1, source_target_pairs={{0,1},{1,0},{2,3},{3,2},{4,5},{5,4},{6,7},{7,6},{8,9},{9,8},{10,11... | collective-permute-start | bytes 3538952 | tf_op jit(solution)/shard_map/ppermute | solution.py:58
  41.6 8.2 %collective-permute-start.11 = (bf16[4,128,1152]{2,1,0:T(8,128)(2,1)S(1)}, bf16[4,128,1152]{2,1,0:T(8,128)(2,1)S(1)}, u32[]{:S(2)}, u32[]{:S(2)}) collective-permute-start(bf16[4,128,1152]{2,1,0:T(8,128)(2,1)S(1)} %collective-permute-done.7.b.refs_0_.side3), channel_id=1, source_target_pairs={{0,1},{1,0},{2,3},{3,2},{4,5},{5,4},{6,7},{7,6},{8,9},{9,8},{10,11... | collective-permute-start | bytes 3538952 | tf_op jit(solution)/shard_map/ppermute | solution.py:58
  42.2 11.8 %collective-permute-start.10 = (bf16[2,128,1152]{2,1,0:T(8,128)(2,1)S(1)}, bf16[2,128,1152]{2,1,0:T(8,128)(2,1)S(1)}, u32[]{:S(2)}, u32[]{:S(2)}) collective-permute-start(bf16[2,128,1152]{2,1,0:T(8,128)(2,1)S(1)} %get-tuple-element.93), channel_id=1, source_target_pairs={{6,0},{97,1},{0,2},{99,3},{2,4},{101,5},{4,6},{103,7},{14,8},{105,... | collective-permute-start | bytes 1769480 | tf_op jit(solution)/shard_map/ppermute | solution.py:53
  43.1 11.0 %collective-permute-start.9 = (bf16[2,128,1152]{2,1,0:T(8,128)(2,1)S(1)}, bf16[2,128,1152]{2,1,0:T(8,128)(2,1)S(1)}, u32[]{:S(2)}, u32[]{:S(2)}) collective-permute-start(bf16[2,128,1152]{2,1,0:T(8,128)(2,1)S(1)} %get-tuple-element.92), channel_id=1, source_target_pairs={{2,0},{33,1},{4,2},{35,3},{6,4},{37,5},{0,6},{39,7},{10,8},{41,9},... | collective-permute-start | bytes 1769480 | tf_op jit(solution)/shard_map/ppermute | solution.py:53
  54.0 2.9 %collective-permute-start.13 = (bf16[2,128,1152]{2,1,0:T(8,128)(2,1)S(1)}, bf16[2,128,1152]{2,1,0:T(8,128)(2,1)S(1)}, u32[]{:S(2)}, u32[]{:S(2)}) collective-permute-start(bf16[2,128,1152]{2,1,0:T(8,128)(2,1)S(1)} %collective-permute-done.9.refs_0_.low), channel_id=1, source_target_pairs={{0,1},{1,0},{2,3},{3,2},{4,5},{5,4},{6,7},{7,6},{8,9},{9,8},{10,11... | collective-permute-start | bytes 1769480 | tf_op jit(solution)/shard_map/ppermute | solution.py:58
  62.9 3.0 %collective-permute-start.16 = (bf16[128,2432]{1,0:T(8,128)(2,1)S(1)}, bf16[128,2432]{1,0:T(8,128)(2,1)S(1)}, u32[]{:S(2)}, u32[]{:S(2)}) collective-permute-start(bf16[128,2432]{1,0:T(8,128)(2,1)S(1)} %get-tuple-element.108), channel_id=1, source_target_pairs={{0,1},{1,0},{2,3},{3,2},{4,5},{5,4},{6,7},{7,6},{8,9},{9,8},{10,11... | collective-permute-start | bytes 1867784 | tf_op jit(solution)/shard_map/ppermute | solution.py:58
  66.4 11.7 %collective-permute-start.17 = (bf16[64,4992]{1,0:T(8,128)(2,1)S(1)}, bf16[64,4992]{1,0:T(8,128)(2,1)S(1)}, u32[]{:S(2)}, u32[]{:S(2)}) collective-permute-start(bf16[64,4992]{1,0:T(8,128)(2,1)S(1)} %get-tuple-element.113), channel_id=1, source_target_pairs={{6,0},{97,1},{0,2},{99,3},{2,4},{101,5},{4,6},{103,7},{14,8},{105,... | collective-permute-start | bytes 1916936 | tf_op jit(solution)/shard_map/ppermute | solution.py:53
  68.3 11.6 %collective-permute-start.18 = (bf16[64,4992]{1,0:T(8,128)(2,1)S(1)}, bf16[64,4992]{1,0:T(8,128)(2,1)S(1)}, u32[]{:S(2)}, u32[]{:S(2)}) collective-permute-start(bf16[64,4992]{1,0:T(8,128)(2,1)S(1)} %get-tuple-element.114), channel_id=1, source_target_pairs={{2,0},{33,1},{4,2},{35,3},{6,4},{37,5},{0,6},{39,7},{10,8},{41,9},... | collective-permute-start | bytes 1916936 | tf_op jit(solution)/shard_map/ppermute | solution.py:53
  73.2 6.8 %collective-permute-start.22 = (bf16[128,2432]{1,0:T(8,128)(2,1)S(1)}, bf16[128,2432]{1,0:T(8,128)(2,1)S(1)}, u32[]{:S(2)}, u32[]{:S(2)}) collective-permute-start(bf16[128,2432]{1,0:T(8,128)(2,1)S(1)} %get-tuple-element.126), channel_id=1, source_target_pairs={{0,1},{1,0},{2,3},{3,2},{4,5},{5,4},{6,7},{7,6},{8,9},{9,8},{10,11... | collective-permute-start | bytes 1867784 | tf_op jit(solution)/shard_map/ppermute | solution.py:58
  77.0 3.9 %collective-permute-start.20 = (bf16[128,2432]{1,0:T(8,128)(2,1)S(1)}, bf16[128,2432]{1,0:T(8,128)(2,1)S(1)}, u32[]{:S(2)}, u32[]{:S(2)}) collective-permute-start(bf16[128,2432]{1,0:T(8,128)(2,1)S(1)} %get-tuple-element.122), channel_id=1, source_target_pairs={{0,1},{1,0},{2,3},{3,2},{4,5},{5,4},{6,7},{7,6},{8,9},{9,8},{10,11... | collective-permute-start | bytes 1867784 | tf_op jit(solution)/shard_map/ppermute | solution.py:58
  81.6 17.8 %collective-permute-start.25 = (bf16[128,4736]{1,0:T(8,128)(2,1)S(1)}, bf16[128,4736]{1,0:T(8,128)(2,1)S(1)}, u32[]{:S(2)}, u32[]{:S(2)}) collective-permute-start(bf16[128,4736]{1,0:T(8,128)(2,1)S(1)} %pair_sum.4), channel_id=1, source_target_pairs={{6,0},{97,1},{0,2},{99,3},{2,4},{101,5},{4,6},{103,7},{14,8},{105,... | collective-permute-start | bytes 3637256 | tf_op jit(solution)/shard_map/ppermute | solution.py:53
  83.4 16.9 %collective-permute-start.26 = (bf16[128,4736]{1,0:T(8,128)(2,1)S(1)}, bf16[128,4736]{1,0:T(8,128)(2,1)S(1)}, u32[]{:S(2)}, u32[]{:S(2)}) collective-permute-start(bf16[128,4736]{1,0:T(8,128)(2,1)S(1)} %pair_sum.5), channel_id=1, source_target_pairs={{2,0},{33,1},{4,2},{35,3},{6,4},{37,5},{0,6},{39,7},{10,8},{41,9},... | collective-permute-start | bytes 3637256 | tf_op jit(solution)/shard_map/ppermute | solution.py:53
  89.3 3.0 %collective-permute-start.24 = (bf16[128,2432]{1,0:T(8,128)(2,1)S(1)}, bf16[128,2432]{1,0:T(8,128)(2,1)S(1)}, u32[]{:S(2)}, u32[]{:S(2)}) collective-permute-start(bf16[128,2432]{1,0:T(8,128)(2,1)S(1)} %get-tuple-element.132), channel_id=1, source_target_pairs={{0,1},{1,0},{2,3},{3,2},{4,5},{5,4},{6,7},{7,6},{8,9},{9,8},{10,11... | collective-permute-start | bytes 1867784 | tf_op jit(solution)/shard_map/ppermute | solution.py:58
  101.7 11.1 %collective-permute-start.27 = (bf16[32,5120]{1,0:T(8,128)(2,1)S(1)}, bf16[32,5120]{1,0:T(8,128)(2,1)S(1)}, u32[]{:S(2)}, u32[]{:S(2)}) collective-permute-start(bf16[32,5120]{1,0:T(8,128)(2,1)S(1)} %get-tuple-element.136), channel_id=1, source_target_pairs={{96,0},{25,1},{98,2},{27,3},{100,4},{29,5},{102,6},{31,7},{104,8},... | collective-permute-start | bytes 983048 | tf_op jit(solution)/shard_map/ppermute | solution.py:53
  104.7 8.7 %collective-permute-start.28 = (bf16[32,5120]{1,0:T(8,128)(2,1)S(1)}, bf16[32,5120]{1,0:T(8,128)(2,1)S(1)}, u32[]{:S(2)}, u32[]{:S(2)}) collective-permute-start(bf16[32,5120]{1,0:T(8,128)(2,1)S(1)} %get-tuple-element.137), channel_id=1, source_target_pairs={{64,0},{17,1},{66,2},{19,3},{68,4},{21,5},{70,6},{23,7},{72,8},{25... | collective-permute-start | bytes 983048 | tf_op jit(solution)/shard_map/ppermute | solution.py:53
  104.7 11.8 %collective-permute-start.29 = (bf16[32,5120]{1,0:T(8,128)(2,1)S(1)}, bf16[32,5120]{1,0:T(8,128)(2,1)S(1)}, u32[]{:S(2)}, u32[]{:S(2)}) collective-permute-start(bf16[32,5120]{1,0:T(8,128)(2,1)S(1)} %get-tuple-element.138), channel_id=1, source_target_pairs={{32,0},{9,1},{34,2},{11,3},{36,4},{13,5},{38,6},{15,7},{40,8},{17,... | collective-permute-start | bytes 983048 | tf_op jit(solution)/shard_map/ppermute | solution.py:53
  117.4 8.7 %collective-permute-start.30 = (f32[8,5632]{1,0:T(8,128)S(1)}, f32[8,5632]{1,0:T(8,128)S(1)}, u32[]{:S(2)}, u32[]{:S(2)}) collective-permute-start(f32[8,5632]{1,0:T(8,128)S(1)} %get-tuple-element.140), channel_id=1, source_target_pairs={{24,0},{7,1},{26,2},{1,3},{28,4},{3,5},{30,6},{5,7},{0,8},{15,9},{... | collective-permute-start | bytes 540680 | tf_op jit(solution)/shard_map/ppermute | solution.py:53
  117.5 8.6 %collective-permute-start.31 = (f32[8,5632]{1,0:T(8,128)S(1)}, f32[8,5632]{1,0:T(8,128)S(1)}, u32[]{:S(2)}, u32[]{:S(2)}) collective-permute-start(f32[8,5632]{1,0:T(8,128)S(1)} %get-tuple-element.141), channel_id=1, source_target_pairs={{16,0},{5,1},{18,2},{7,3},{20,4},{1,5},{22,6},{3,7},{24,8},{13,9},... | collective-permute-start | bytes 540680 | tf_op jit(solution)/shard_map/ppermute | solution.py:53
  119.8 7.2 %collective-permute-start.32 = (f32[8,5632]{1,0:T(8,128)S(1)}, f32[8,5632]{1,0:T(8,128)S(1)}, u32[]{:S(2)}, u32[]{:S(2)}) collective-permute-start(f32[8,5632]{1,0:T(8,128)S(1)} %get-tuple-element.142), channel_id=1, source_target_pairs={{8,0},{3,1},{10,2},{5,3},{12,4},{7,5},{14,6},{1,7},{16,8},{11,9},{... | collective-permute-start | bytes 540680 | tf_op jit(solution)/shard_map/ppermute | solution.py:53
  127.2 6.5 %collective-permute-start.34 = (f32[8,1024]{1,0:T(8,128)S(1)}, f32[8,1024]{1,0:T(8,128)S(1)}, u32[]{:S(2)}, u32[]{:S(2)}) collective-permute-start(f32[8,1024]{1,0:T(8,128)S(1)} %get-tuple-element.144.refs_0_), channel_id=1, source_target_pairs={{2,0},{33,1},{4,2},{35,3},{6,4},{37,5},{0,6},{39,7},{10,8},{41,9},... | collective-permute-start | bytes 98312 | tf_op jit(solution)/shard_map/ppermute | solution.py:53
  129.0 5.4 %collective-permute-start.35 = (f32[8,1024]{1,0:T(8,128)S(1)}, f32[8,1024]{1,0:T(8,128)S(1)}, u32[]{:S(2)}, u32[]{:S(2)}) collective-permute-start(f32[8,1024]{1,0:T(8,128)S(1)} %get-tuple-element.144.refs_0_), channel_id=1, source_target_pairs={{4,0},{65,1},{6,2},{67,3},{0,4},{69,5},{2,6},{71,7},{12,8},{73,9},... | collective-permute-start | bytes 98312 | tf_op jit(solution)/shard_map/ppermute | solution.py:53
  131.1 4.1 %collective-permute-start.36 = (f32[8,1024]{1,0:T(8,128)S(1)}, f32[8,1024]{1,0:T(8,128)S(1)}, u32[]{:S(2)}, u32[]{:S(2)}) collective-permute-start(f32[8,1024]{1,0:T(8,128)S(1)} %get-tuple-element.144.refs_0_), channel_id=1, source_target_pairs={{6,0},{97,1},{0,2},{99,3},{2,4},{101,5},{4,6},{103,7},{14,8},{105,... | collective-permute-start | bytes 98312 | tf_op jit(solution)/shard_map/ppermute | solution.py:53
  135.3 4.5 %collective-permute-start.37 = (f32[4,8,1024]{2,1,0:T(8,128)S(1)}, f32[4,8,1024]{2,1,0:T(8,128)S(1)}, u32[]{:S(2)}, u32[]{:S(2)}) collective-permute-start(f32[4,8,1024]{2,1,0:T(8,128)S(1)} %collect.3.own), channel_id=1, source_target_pairs={{0,1},{1,0},{2,3},{3,2},{4,5},{5,4},{6,7},{7,6},{8,9},{9,8},{10,11... | collective-permute-start | bytes 393224 | tf_op jit(solution)/shard_map/ppermute | solution.py:58
  135.4 11.5 %collective-permute-start.33 = (f32[8,128]{1,0:T(8,128)S(1)}, f32[8,128]{1,0:T(8,128)S(1)}, u32[]{:S(2)}, u32[]{:S(2)}) collective-permute-start(f32[8,128]{1,0:T(8,128)S(1)} %get-tuple-element.143), channel_id=1, source_target_pairs={{0,0},{1,16},{2,32},{3,17},{4,64},{5,18},{6,96},{7,19},{8,1},{9,20... | collective-permute-start | bytes 12296 | tf_op jit(solution)/shard_map/ppermute | solution.py:547
  (12 other events, 88.8 us)

commit v3 on v2

--- a/solution.py
+++ b/solution.py
@@ -238,7 +238,7 @@
     lat = dec.shape[0]
     vmem = pl.BlockSpec(memory_space=pltpu.VMEM)
     return pl.pallas_call(
-        functools.partial(decode_kernel, step, 768),
+        functools.partial(decode_kernel, step, 1152 if step else 256),
         in_specs=[pl.BlockSpec(memory_space=pltpu.SMEM)] + [vmem] * 4,
         out_specs=[vmem] * 3,
         scratch_shapes=[pltpu.VMEM((256, lat), BF16)],

time: 148 us -> 149 us (level)
  Pallas kernels: 46.9 us -> 49.7 us
  waiting for transfers between devices: 52.5 us -> 50.1 us
    ppermute x23, waiting for transfers between devices: 41.8 us -> 38.9 us  [pull(): return lax.ppermute(value, AXES, pull_perm(axis0, axis1, step))]
    pallas_call x4, Pallas kernels: 14.6 us -> 17.4 us  [decode(): pl.pallas_call(functools.partial(decode_kernel, step, 1152 if step else 2...]
  transfers between devices with their start and end apart: 38 -> 38, of which waited for: 23 -> 22; matrix products, arithmetic and copies ran while one was open for 2% -> 2% of each run, Pallas kernels for 25% -> 27%
where the time goes in v3:
time: 149 us; the launch traced here: 148 us
  waiting for transfers between devices  50.1 us (34%)
  Pallas kernels  49.7 us (33%)
  starting transfers between devices  44 us (30%)
  local copies, waits for them, and re-layouts  3.29 us (2%)
    ppermute x23, waiting for transfers between devices, pull(): return lax.ppermute(value, AXES, pull_perm(axis0, axis1, step))  38.9 us
    ppermute x23, starting transfers between devices, pull(): return lax.ppermute(value, AXES, pull_perm(axis0, axis1, step))  36.3 us
    pallas_call x4, Pallas kernels, decode(): pl.pallas_call(functools.partial(decode_kernel, step, 1152 if step else 2...  17.4 us
    pallas_call x5, Pallas kernels, encode(): pl.pallas_call(functools.partial(encode_kernel, stage, which, 256), in_sp...  17.2 us
    pallas_call x2, Pallas kernels, load(): pl.pallas_call(load_kernel, in_specs=[pl.BlockSpec(memory_space=pltpu.HBM...  7.6 us
    pallas_call x12, Pallas kernels, small_call(): pl.pallas_call(kernel, in_specs=[smem] * scalars + [vmem] * (len(args) -...  7.57 us
    ppermute x14, waiting for transfers between devices, swap(): return lax.ppermute(value, AXES, pairs)  6.45 us
    ppermute x1, waiting for transfers between devices, on_device(): err = lax.ppermute(err, AXES, owners)  4.71 us
  transfers between devices with their start and end apart: 38, of which 22 were waited for; matrix products, arithmetic and copies ran while one was open for 2% of the time, Pallas kernels for 27%

profile of v3, /device:TPU:26, one launch (start us, length us, event | category | flops | bytes accessed | tf_op | source)
XLA Modules:
  0.0 148.3 jit_solution(15908627320892262724)
XLA Ops:
  0.6 4.1 %collective-permute-start = (bf16[128,288]{0,1:T(8,128)(2,1)}, bf16[128,288]{0,1:T(8,128)(2,1)S(1)}, u32[]{:S(2)}, u32[]{:S(2)}) collective-permute-start(bf16[128,288]{0,1:T(8,128)(2,1)} %param.9), channel_id=1, source_target_pairs={{8,0},{9,1},{10,2},{11,3},{12,4},{13,5},{14,6},{15,7},{16,8},{17,9... | collective-permute-start | bytes 221192 | tf_op jit(solution)/shard_map/ppermute | solution.py:53
  8.3 2.7 %collective-permute-done.1 = bf16[128,288]{0,1:T(8,128)(2,1)S(1)} collective-permute-done((bf16[128,288]{0,1:T(8,128)(2,1)}, bf16[128,288]{0,1:T(8,128)(2,1)S(1)}, u32[]{:S(2)}, u32[]{:S(2)}) %collective-permute-start.1) | collective-permute-done | bytes 73760 | tf_op jit(solution)/shard_map/ppermute | solution.py:53
  13.6 2.2 %collective-permute-start.5 = (bf16[128,1152]{1,0:T(8,128)(2,1)S(1)}, bf16[128,1152]{1,0:T(8,128)(2,1)S(1)}, u32[]{:S(2)}, u32[]{:S(2)}) collective-permute-start(bf16[128,1152]{1,0:T(8,128)(2,1)S(1)} %settle.1.refs_0_), channel_id=1, source_target_pairs={{96,0},{7,1},{98,2},{1,3},{100,4},{3,5},{102,6},{5,7},{104,8},{15,... | collective-permute-start | bytes 884744 | tf_op jit(solution)/shard_map/ppermute | solution.py:53
  15.8 3.8 %load.2.refs_2_ = bf16[4608,1024]{1,0:T(8,128)(2,1)S(1)} custom-call(bf16[4608,1024]{1,0:T(8,128)(2,1)} %source), custom_call_target="tpu_custom_call" | custom-call | flops 1000000 | tf_op jit(solution)/shard_map/load/pallas_call | solution.py:80
  19.6 3.8 %load.3.dec = bf16[1024,4608]{1,0:T(8,128)(2,1)S(1)} custom-call(bf16[1024,4608]{1,0:T(8,128)(2,1)} %source.1), custom_call_target="tpu_custom_call" | custom-call | flops 1000000 | tf_op jit(solution)/shard_map/load/pallas_call | solution.py:80
  26.9 4.1 %encode.5 = (bf16[128,1024]{1,0:T(8,128)(2,1)S(1)}, f32[512,1024]{1,0:T(8,128)S(1)}) custom-call(s32[7]{0:T(128)S(1)} %stack.55.where, bf16[4,128,1152]{2,1,0:T(8,128)(2,1)S(1)} %collect.2.refs_0_.block, bf16[4,128,1152]{2,1,0:T(8,128)(2,1)S(1)} %collective-permute-done.8.refs_1_, bf16[4608,1024]{1,0:T(8,128)(2,1)S(1)} %load.2.refs_2_, ...), custom_call_target="tpu_custom_call" | custom-call | flops 1000000 | tf_op jit(solution)/shard_map/encode/pallas_call | solution.py:184
  31.1 9.3 %collective-permute-done.6.a.refs_0_.side1 = bf16[4,128,1152]{2,1,0:T(8,128)(2,1)S(1)} collective-permute-done((bf16[4,128,1152]{2,1,0:T(8,128)(2,1)S(1)}, bf16[4,128,1152]{2,1,0:T(8,128)(2,1)S(1)}, u32[]{:S(2)}, u32[]{:S(2)}) %collective-permute-start.6) | collective-permute-done | bytes 1179680 | tf_op jit(solution)/shard_map/ppermute | solution.py:53
  43.1 2.6 %collective-permute-start.9 = (bf16[2,128,1152]{2,1,0:T(8,128)(2,1)S(1)}, bf16[2,128,1152]{2,1,0:T(8,128)(2,1)S(1)}, u32[]{:S(2)}, u32[]{:S(2)}) collective-permute-start(bf16[2,128,1152]{2,1,0:T(8,128)(2,1)S(1)} %get-tuple-element.92), channel_id=1, source_target_pairs={{2,0},{33,1},{4,2},{35,3},{6,4},{37,5},{0,6},{39,7},{10,8},{41,9},... | collective-permute-start | bytes 1769480 | tf_op jit(solution)/shard_map/ppermute | solution.py:53
  45.6 4.2 %encode.6 = (bf16[128,1024]{1,0:T(8,128)(2,1)S(1)}, f32[512,1024]{1,0:T(8,128)S(1)}) custom-call(s32[7]{0:T(128)S(1)} %stack.55.where, bf16[4,128,1152]{2,1,0:T(8,128)(2,1)S(1)} %collective-permute-done.6.a.refs_0_.side1, bf16[4,128,1152]{2,1,0:T(8,128)(2,1)S(1)} %collective-permute-done.12.refs_1_, ...), custom_call_target="tpu_custom_call", output_to_operand_aliasing={{1}: (6, {})} | custom-call | flops 1000000 | tf_op jit(solution)/shard_map/encode/pallas_call | solution.py:184
  49.8 4.2 %encode.7 = (bf16[128,1024]{1,0:T(8,128)(2,1)S(1)}, f32[512,1024]{1,0:T(8,128)S(1)}) custom-call(s32[7]{0:T(128)S(1)} %stack.55.where, bf16[4,128,1152]{2,1,0:T(8,128)(2,1)S(1)} %collective-permute-done.7.b.refs_0_.side3, bf16[4,128,1152]{2,1,0:T(8,128)(2,1)S(1)} %collective-permute-done.11.refs_1_, ...), custom_call_target="tpu_custom_call", output_to_operand_aliasing={{1}: (6, {})} | custom-call | flops 1000000 | tf_op jit(solution)/shard_map/encode/pallas_call | solution.py:184
  54.6 2.3 %encode.8 = (bf16[128,1024]{1,0:T(8,128)(2,1)S(1)}, bf16[512,1024]{1,0:T(8,128)(2,1)S(1)}) custom-call(s32[7]{0:T(128)S(1)} %stack.55.where, bf16[2,128,1152]{2,1,0:T(8,128)(2,1)S(1)} %collective-permute-done.9.refs_0_.low, bf16[2,128,1152]{2,1,0:T(8,128)(2,1)S(1)} %collective-permute-done.10.refs_1_.high, bf16[4608,1024]{1,0:T(8,128)(2,1)S(1)} %load.2.refs_2_, ...), custom_call_target="tpu_custom_call" | custom-call | flops 1000000 | tf_op jit(solution)/shard_map/encode/pallas_call | solution.py:184
  57.1 2.4 %encode.9 = (bf16[128,1024]{1,0:T(8,128)(2,1)S(1)}, bf16[512,1024]{1,0:T(8,128)(2,1)S(1)}) custom-call(s32[7]{0:T(128)S(1)} %stack.55.where, bf16[2,128,1152]{2,1,0:T(8,128)(2,1)S(1)} %collective-permute-done.13.refs_0_, bf16[2,128,1152]{2,1,0:T(8,128)(2,1)S(1)} %collective-permute-done.14.refs_1_, ...), custom_call_target="tpu_custom_call", output_to_operand_aliasing={{0}: (7, {}), {1}: (8, {})} | custom-call | flops 1000000 | tf_op jit(solution)/shard_map/encode/pallas_call | solution.py:184
  59.5 3.7 %decode.4 = (bf16[128,4736]{1,0:T(8,128)(2,1)S(1)}, bf16[128,2304]{1,0:T(8,128)(2,1)S(1)}, bf16[128,2432]{1,0:T(8,128)(2,1)S(1)}) custom-call(s32[7]{0:T(128)S(1)} %stack.55.where, bf16[128,1024]{1,0:T(8,128)(2,1)S(1)} %get-tuple-element.102.xa.refs_2_, bf16[4,128,1024]{2,1,0:T(8,128)(2,1)S(1)} %bitcast.30, bf16[1024,4608]{1,0:T(8,128)(2,1)S(1)} %load.3.dec, ...), custom_call_target="tpu_custom_call" | custom-call | flops 1000000 | tf_op jit(solution)/shard_map/decode/pallas_call | solution.py:240
  63.7 2.4 %collective-permute-done.15.b0 = bf16[128,2304]{1,0:T(8,128)(2,1)S(1)} collective-permute-done((bf16[128,2304]{1,0:T(8,128)(2,1)S(1)}, bf16[128,2304]{1,0:T(8,128)(2,1)S(1)}, u32[]{:S(2)}, u32[]{:S(2)}) %collective-permute-start.15) | collective-permute-done | bytes 589856 | tf_op jit(solution)/shard_map/ppermute | solution.py:58
  66.7 1.9 %collective-permute-start.17 = (bf16[64,4992]{1,0:T(8,128)(2,1)S(1)}, bf16[64,4992]{1,0:T(8,128)(2,1)S(1)}, u32[]{:S(2)}, u32[]{:S(2)}) collective-permute-start(bf16[64,4992]{1,0:T(8,128)(2,1)S(1)} %get-tuple-element.113), channel_id=1, source_target_pairs={{6,0},{97,1},{0,2},{99,3},{2,4},{101,5},{4,6},{103,7},{14,8},{105,... | collective-permute-start | bytes 1916936 | tf_op jit(solution)/shard_map/ppermute | solution.py:53
  68.6 1.7 %collective-permute-start.18 = (bf16[64,4992]{1,0:T(8,128)(2,1)S(1)}, bf16[64,4992]{1,0:T(8,128)(2,1)S(1)}, u32[]{:S(2)}, u32[]{:S(2)}) collective-permute-start(bf16[64,4992]{1,0:T(8,128)(2,1)S(1)} %get-tuple-element.114), channel_id=1, source_target_pairs={{2,0},{33,1},{4,2},{35,3},{6,4},{37,5},{0,6},{39,7},{10,8},{41,9},... | collective-permute-start | bytes 1916936 | tf_op jit(solution)/shard_map/ppermute | solution.py:53
  70.3 3.7 %decode.6 = (bf16[128,4736]{1,0:T(8,128)(2,1)S(1)}, bf16[128,2304]{1,0:T(8,128)(2,1)S(1)}, bf16[128,2432]{1,0:T(8,128)(2,1)S(1)}) custom-call(s32[7]{0:T(128)S(1)} %stack.55.where, bf16[128,1024]{1,0:T(8,128)(2,1)S(1)} %get-tuple-element.117.xa.refs_3_, bf16[4,128,1024]{2,1,0:T(8,128)(2,1)S(1)} %bitcast.31, bf16[1024,4608]{1,0:T(8,128)(2,1)S(1)} %load.3.dec, ...), custom_call_target="tpu_custom_call" | custom-call | flops 1000000 | tf_op jit(solution)/shard_map/decode/pallas_call | solution.py:240
  74.0 3.7 %decode.5 = (bf16[128,4736]{1,0:T(8,128)(2,1)S(1)}, bf16[128,2304]{1,0:T(8,128)(2,1)S(1)}, bf16[128,2432]{1,0:T(8,128)(2,1)S(1)}) custom-call(s32[7]{0:T(128)S(1)} %stack.55.where, bf16[128,1024]{1,0:T(8,128)(2,1)S(1)} %get-tuple-element.115.xa.refs_1_, bf16[4,128,1024]{2,1,0:T(8,128)(2,1)S(1)} %bitcast.32, bf16[1024,4608]{1,0:T(8,128)(2,1)S(1)} %load.3.dec, ...), custom_call_target="tpu_custom_call" | custom-call | flops 1000000 | tf_op jit(solution)/shard_map/decode/pallas_call | solution.py:240
  85.4 6.4 %decode.7 = (bf16[128,4736]{1,0:T(8,128)(2,1)S(1)}, bf16[128,2304]{1,0:T(8,128)(2,1)S(1)}, bf16[128,2432]{1,0:T(8,128)(2,1)S(1)}) custom-call(s32[7]{0:T(128)S(1)} %stack.55.where, bf16[128,1024]{1,0:T(8,128)(2,1)S(1)} %get-tuple-element.129.xa.refs_0_, bf16[4,128,1024]{2,1,0:T(8,128)(2,1)S(1)} %bitcast.33, bf16[1024,4608]{1,0:T(8,128)(2,1)S(1)} %load.3.dec, ...), custom_call_target="tpu_custom_call" | custom-call | flops 1000000 | tf_op jit(solution)/shard_map/decode/pallas_call | solution.py:240
  92.4 2.4 %collective-permute-done.23.b0 = bf16[128,2304]{1,0:T(8,128)(2,1)S(1)} collective-permute-done((bf16[128,2304]{1,0:T(8,128)(2,1)S(1)}, bf16[128,2304]{1,0:T(8,128)(2,1)S(1)}, u32[]{:S(2)}, u32[]{:S(2)}) %collective-permute-start.23) | collective-permute-done | bytes 589856 | tf_op jit(solution)/shard_map/ppermute | solution.py:58
  94.8 5.1 %collective-permute-done.25.g1 = bf16[128,4736]{1,0:T(8,128)(2,1)S(1)} collective-permute-done((bf16[128,4736]{1,0:T(8,128)(2,1)S(1)}, bf16[128,4736]{1,0:T(8,128)(2,1)S(1)}, u32[]{:S(2)}, u32[]{:S(2)}) %collective-permute-start.25) | collective-permute-done | bytes 1212448 | tf_op jit(solution)/shard_map/ppermute | solution.py:53
  102.2 3.0 %collective-permute-start.27 = (bf16[32,5120]{1,0:T(8,128)(2,1)S(1)}, bf16[32,5120]{1,0:T(8,128)(2,1)S(1)}, u32[]{:S(2)}, u32[]{:S(2)}) collective-permute-start(bf16[32,5120]{1,0:T(8,128)(2,1)S(1)} %get-tuple-element.136), channel_id=1, source_target_pairs={{96,0},{25,1},{98,2},{27,3},{100,4},{29,5},{102,6},{31,7},{104,8},... | collective-permute-start | bytes 983048 | tf_op jit(solution)/shard_map/ppermute | solution.py:53
  106.2 7.2 %collective-permute-done.27.g1 = bf16[32,5120]{1,0:T(8,128)(2,1)S(1)} collective-permute-done((bf16[32,5120]{1,0:T(8,128)(2,1)S(1)}, bf16[32,5120]{1,0:T(8,128)(2,1)S(1)}, u32[]{:S(2)}, u32[]{:S(2)}) %collective-permute-start.27) | collective-permute-done | bytes 327712 | tf_op jit(solution)/shard_map/ppermute | solution.py:53
  113.9 3.1 %collective-permute-done.29.g3 = bf16[32,5120]{1,0:T(8,128)(2,1)S(1)} collective-permute-done((bf16[32,5120]{1,0:T(8,128)(2,1)S(1)}, bf16[32,5120]{1,0:T(8,128)(2,1)S(1)}, u32[]{:S(2)}, u32[]{:S(2)}) %collective-permute-start.29) | collective-permute-done | bytes 327712 | tf_op jit(solution)/shard_map/ppermute | solution.py:53
  118.3 2.3 %collective-permute-start.31 = (f32[8,5632]{1,0:T(8,128)S(1)}, f32[8,5632]{1,0:T(8,128)S(1)}, u32[]{:S(2)}, u32[]{:S(2)}) collective-permute-start(f32[8,5632]{1,0:T(8,128)S(1)} %get-tuple-element.141), channel_id=1, source_target_pairs={{16,0},{5,1},{18,2},{7,3},{20,4},{1,5},{22,6},{3,7},{24,8},{13,9},... | collective-permute-start | bytes 540680 | tf_op jit(solution)/shard_map/ppermute | solution.py:53
  123.0 4.0 %collective-permute-done.30.g1 = f32[8,5632]{1,0:T(8,128)S(1)} collective-permute-done((f32[8,5632]{1,0:T(8,128)S(1)}, f32[8,5632]{1,0:T(8,128)S(1)}, u32[]{:S(2)}, u32[]{:S(2)}) %collective-permute-start.30) | collective-permute-done | bytes 180256 | tf_op jit(solution)/shard_map/ppermute | solution.py:53
  127.9 1.8 %collective-permute-start.34 = (f32[8,1024]{1,0:T(8,128)S(1)}, f32[8,1024]{1,0:T(8,128)S(1)}, u32[]{:S(2)}, u32[]{:S(2)}) collective-permute-start(f32[8,1024]{1,0:T(8,128)S(1)} %get-tuple-element.144.refs_0_), channel_id=1, source_target_pairs={{2,0},{33,1},{4,2},{35,3},{6,4},{37,5},{0,6},{39,7},{10,8},{41,9},... | collective-permute-start | bytes 98312 | tf_op jit(solution)/shard_map/ppermute | solution.py:53
  129.8 2.2 %collective-permute-start.35 = (f32[8,1024]{1,0:T(8,128)S(1)}, f32[8,1024]{1,0:T(8,128)S(1)}, u32[]{:S(2)}, u32[]{:S(2)}) collective-permute-start(f32[8,1024]{1,0:T(8,128)S(1)} %get-tuple-element.144.refs_0_), channel_id=1, source_target_pairs={{4,0},{65,1},{6,2},{67,3},{0,4},{69,5},{2,6},{71,7},{12,8},{73,9},... | collective-permute-start | bytes 98312 | tf_op jit(solution)/shard_map/ppermute | solution.py:53
  131.9 2.5 %collective-permute-start.36 = (f32[8,1024]{1,0:T(8,128)S(1)}, f32[8,1024]{1,0:T(8,128)S(1)}, u32[]{:S(2)}, u32[]{:S(2)}) collective-permute-start(f32[8,1024]{1,0:T(8,128)S(1)} %get-tuple-element.144.refs_0_), channel_id=1, source_target_pairs={{6,0},{97,1},{0,2},{99,3},{2,4},{101,5},{4,6},{103,7},{14,8},{105,... | collective-permute-start | bytes 98312 | tf_op jit(solution)/shard_map/ppermute | solution.py:53
  136.2 4.2 %collective-permute-start.33 = (f32[8,128]{1,0:T(8,128)S(1)}, f32[8,128]{1,0:T(8,128)S(1)}, u32[]{:S(2)}, u32[]{:S(2)}) collective-permute-start(f32[8,128]{1,0:T(8,128)S(1)} %get-tuple-element.143), channel_id=1, source_target_pairs={{0,0},{1,16},{2,32},{3,17},{4,64},{5,18},{6,96},{7,19},{8,1},{9,20... | collective-permute-start | bytes 12296 | tf_op jit(solution)/shard_map/ppermute | solution.py:547
  140.6 2.4 %finish.1 = (f32[64,1024]{1,0:T(8,128)}, f32[1,64]{1,0:T(1,128)}, f32[1,128]{1,0:T(1,128)}) custom-call(s32[7]{0:T(128)S(1)} %stack.55.where, f32[4,8,1024]{2,1,0:T(8,128)S(1)} %collect.3.own, f32[4,8,1024]{2,1,0:T(8,128)S(1)} %collective-permute-done.37.oth, s32[1024,64]{1,0:T(8,128)S(1)} %copy.24.labels, f32[1,64]{1,0:T(1,128)S(1)} %bitcast.45, ...), custom_call_target="tpu_custom_call" | custom-call | flops 1000000 | tf_op jit(solution)/shard_map/finish/pallas_call | solution.py:255
  143.0 4.7 %collective-permute-done.33 = f32[8,128]{1,0:T(8,128)S(1)} collective-permute-done((f32[8,128]{1,0:T(8,128)S(1)}, f32[8,128]{1,0:T(8,128)S(1)}, u32[]{:S(2)}, u32[]{:S(2)}) %collective-permute-start.33) | collective-permute-done | bytes 4128 | tf_op jit(solution)/shard_map/ppermute | solution.py:547
  (95 shorter events, 33.4 us)
Async XLA Ops:
  0.6 7.6 %collective-permute-start = (bf16[128,288]{0,1:T(8,128)(2,1)}, bf16[128,288]{0,1:T(8,128)(2,1)S(1)}, u32[]{:S(2)}, u32[]{:S(2)}) collective-permute-start(bf16[128,288]{0,1:T(8,128)(2,1)} %param.9), channel_id=1, source_target_pairs={{8,0},{9,1},{10,2},{11,3},{12,4},{13,5},{14,6},{15,7},{16,8},{17,9... | collective-permute-start | bytes 221192 | tf_op jit(solution)/shard_map/ppermute | solution.py:53
  4.7 6.3 %collective-permute-start.1 = (bf16[128,288]{0,1:T(8,128)(2,1)}, bf16[128,288]{0,1:T(8,128)(2,1)S(1)}, u32[]{:S(2)}, u32[]{:S(2)}) collective-permute-start(bf16[128,288]{0,1:T(8,128)(2,1)} %param.9), channel_id=1, source_target_pairs={{16,0},{17,1},{18,2},{19,3},{20,4},{21,5},{22,6},{23,7},{24,8},{25... | collective-permute-start | bytes 221192 | tf_op jit(solution)/shard_map/ppermute | solution.py:53
  4.7 6.7 %collective-permute-start.2 = (bf16[128,288]{0,1:T(8,128)(2,1)}, bf16[128,288]{0,1:T(8,128)(2,1)S(1)}, u32[]{:S(2)}, u32[]{:S(2)}) collective-permute-start(bf16[128,288]{0,1:T(8,128)(2,1)} %param.9), channel_id=1, source_target_pairs={{24,0},{25,1},{26,2},{27,3},{28,4},{29,5},{30,6},{31,7},{0,8},{1,9... | collective-permute-start | bytes 221192 | tf_op jit(solution)/shard_map/ppermute | solution.py:53
  11.9 11.6 %collective-permute-start.3 = (bf16[128,1152]{1,0:T(8,128)(2,1)S(1)}, bf16[128,1152]{1,0:T(8,128)(2,1)S(1)}, u32[]{:S(2)}, u32[]{:S(2)}) collective-permute-start(bf16[128,1152]{1,0:T(8,128)(2,1)S(1)} %settle.1.refs_0_), channel_id=1, source_target_pairs={{32,0},{3,1},{34,2},{5,3},{36,4},{7,5},{38,6},{1,7},{40,8},{11,9},... | collective-permute-start | bytes 884744 | tf_op jit(solution)/shard_map/ppermute | solution.py:53
  12.7 10.8 %collective-permute-start.4 = (bf16[128,1152]{1,0:T(8,128)(2,1)S(1)}, bf16[128,1152]{1,0:T(8,128)(2,1)S(1)}, u32[]{:S(2)}, u32[]{:S(2)}) collective-permute-start(bf16[128,1152]{1,0:T(8,128)(2,1)S(1)} %settle.1.refs_0_), channel_id=1, source_target_pairs={{64,0},{5,1},{66,2},{7,3},{68,4},{1,5},{70,6},{3,7},{72,8},{13,9},... | collective-permute-start | bytes 884744 | tf_op jit(solution)/shard_map/ppermute | solution.py:53
  13.6 10.3 %collective-permute-start.5 = (bf16[128,1152]{1,0:T(8,128)(2,1)S(1)}, bf16[128,1152]{1,0:T(8,128)(2,1)S(1)}, u32[]{:S(2)}, u32[]{:S(2)}) collective-permute-start(bf16[128,1152]{1,0:T(8,128)(2,1)S(1)} %settle.1.refs_0_), channel_id=1, source_target_pairs={{96,0},{7,1},{98,2},{1,3},{100,4},{3,5},{102,6},{5,7},{104,8},{15,... | collective-permute-start | bytes 884744 | tf_op jit(solution)/shard_map/ppermute | solution.py:53
  24.1 16.3 %collective-permute-start.6 = (bf16[4,128,1152]{2,1,0:T(8,128)(2,1)S(1)}, bf16[4,128,1152]{2,1,0:T(8,128)(2,1)S(1)}, u32[]{:S(2)}, u32[]{:S(2)}) collective-permute-start(bf16[4,128,1152]{2,1,0:T(8,128)(2,1)S(1)} %collect.2.refs_0_.block), channel_id=1, source_target_pairs={{2,0},{33,1},{4,2},{35,3},{6,4},{37,5},{0,6},{39,7},{10,8},{41,9},... | collective-permute-start | bytes 3538952 | tf_op jit(solution)/shard_map/ppermute | solution.py:53
  24.7 16.9 %collective-permute-start.7 = (bf16[4,128,1152]{2,1,0:T(8,128)(2,1)S(1)}, bf16[4,128,1152]{2,1,0:T(8,128)(2,1)S(1)}, u32[]{:S(2)}, u32[]{:S(2)}) collective-permute-start(bf16[4,128,1152]{2,1,0:T(8,128)(2,1)S(1)} %collect.2.refs_0_.block), channel_id=1, source_target_pairs={{6,0},{97,1},{0,2},{99,3},{2,4},{101,5},{4,6},{103,7},{14,8},{105,... | collective-permute-start | bytes 3538952 | tf_op jit(solution)/shard_map/ppermute | solution.py:53
  41.6 4.0 %collective-permute-start.12 = (bf16[4,128,1152]{2,1,0:T(8,128)(2,1)S(1)}, bf16[4,128,1152]{2,1,0:T(8,128)(2,1)S(1)}, u32[]{:S(2)}, u32[]{:S(2)}) collective-permute-start(bf16[4,128,1152]{2,1,0:T(8,128)(2,1)S(1)} %collective-permute-done.6.a.refs_0_.side1), channel_id=1, source_target_pairs={{0,1},{1,0},{2,3},{3,2},{4,5},{5,4},{6,7},{7,6},{8,9},{9,8},{10,11... | collective-permute-start | bytes 3538952 | tf_op jit(solution)/shard_map/ppermute | solution.py:58
  41.6 8.2 %collective-permute-start.11 = (bf16[4,128,1152]{2,1,0:T(8,128)(2,1)S(1)}, bf16[4,128,1152]{2,1,0:T(8,128)(2,1)S(1)}, u32[]{:S(2)}, u32[]{:S(2)}) collective-permute-start(bf16[4,128,1152]{2,1,0:T(8,128)(2,1)S(1)} %collective-permute-done.7.b.refs_0_.side3), channel_id=1, source_target_pairs={{0,1},{1,0},{2,3},{3,2},{4,5},{5,4},{6,7},{7,6},{8,9},{9,8},{10,11... | collective-permute-start | bytes 3538952 | tf_op jit(solution)/shard_map/ppermute | solution.py:58
  42.2 11.8 %collective-permute-start.10 = (bf16[2,128,1152]{2,1,0:T(8,128)(2,1)S(1)}, bf16[2,128,1152]{2,1,0:T(8,128)(2,1)S(1)}, u32[]{:S(2)}, u32[]{:S(2)}) collective-permute-start(bf16[2,128,1152]{2,1,0:T(8,128)(2,1)S(1)} %get-tuple-element.93), channel_id=1, source_target_pairs={{6,0},{97,1},{0,2},{99,3},{2,4},{101,5},{4,6},{103,7},{14,8},{105,... | collective-permute-start | bytes 1769480 | tf_op jit(solution)/shard_map/ppermute | solution.py:53
  43.1 11.0 %collective-permute-start.9 = (bf16[2,128,1152]{2,1,0:T(8,128)(2,1)S(1)}, bf16[2,128,1152]{2,1,0:T(8,128)(2,1)S(1)}, u32[]{:S(2)}, u32[]{:S(2)}) collective-permute-start(bf16[2,128,1152]{2,1,0:T(8,128)(2,1)S(1)} %get-tuple-element.92), channel_id=1, source_target_pairs={{2,0},{33,1},{4,2},{35,3},{6,4},{37,5},{0,6},{39,7},{10,8},{41,9},... | collective-permute-start | bytes 1769480 | tf_op jit(solution)/shard_map/ppermute | solution.py:53
  63.1 3.0 %collective-permute-start.16 = (bf16[128,2432]{1,0:T(8,128)(2,1)S(1)}, bf16[128,2432]{1,0:T(8,128)(2,1)S(1)}, u32[]{:S(2)}, u32[]{:S(2)}) collective-permute-start(bf16[128,2432]{1,0:T(8,128)(2,1)S(1)} %get-tuple-element.108), channel_id=1, source_target_pairs={{0,1},{1,0},{2,3},{3,2},{4,5},{5,4},{6,7},{7,6},{8,9},{9,8},{10,11... | collective-permute-start | bytes 1867784 | tf_op jit(solution)/shard_map/ppermute | solution.py:58
  66.7 11.7 %collective-permute-start.17 = (bf16[64,4992]{1,0:T(8,128)(2,1)S(1)}, bf16[64,4992]{1,0:T(8,128)(2,1)S(1)}, u32[]{:S(2)}, u32[]{:S(2)}) collective-permute-start(bf16[64,4992]{1,0:T(8,128)(2,1)S(1)} %get-tuple-element.113), channel_id=1, source_target_pairs={{6,0},{97,1},{0,2},{99,3},{2,4},{101,5},{4,6},{103,7},{14,8},{105,... | collective-permute-start | bytes 1916936 | tf_op jit(solution)/shard_map/ppermute | solution.py:53
  68.6 11.6 %collective-permute-start.18 = (bf16[64,4992]{1,0:T(8,128)(2,1)S(1)}, bf16[64,4992]{1,0:T(8,128)(2,1)S(1)}, u32[]{:S(2)}, u32[]{:S(2)}) collective-permute-start(bf16[64,4992]{1,0:T(8,128)(2,1)S(1)} %get-tuple-element.114), channel_id=1, source_target_pairs={{2,0},{33,1},{4,2},{35,3},{6,4},{37,5},{0,6},{39,7},{10,8},{41,9},... | collective-permute-start | bytes 1916936 | tf_op jit(solution)/shard_map/ppermute | solution.py:53
  74.0 6.9 %collective-permute-start.22 = (bf16[128,2432]{1,0:T(8,128)(2,1)S(1)}, bf16[128,2432]{1,0:T(8,128)(2,1)S(1)}, u32[]{:S(2)}, u32[]{:S(2)}) collective-permute-start(bf16[128,2432]{1,0:T(8,128)(2,1)S(1)} %get-tuple-element.126), channel_id=1, source_target_pairs={{0,1},{1,0},{2,3},{3,2},{4,5},{5,4},{6,7},{7,6},{8,9},{9,8},{10,11... | collective-permute-start | bytes 1867784 | tf_op jit(solution)/shard_map/ppermute | solution.py:58
  77.7 3.9 %collective-permute-start.20 = (bf16[128,2432]{1,0:T(8,128)(2,1)S(1)}, bf16[128,2432]{1,0:T(8,128)(2,1)S(1)}, u32[]{:S(2)}, u32[]{:S(2)}) collective-permute-start(bf16[128,2432]{1,0:T(8,128)(2,1)S(1)} %get-tuple-element.122), channel_id=1, source_target_pairs={{0,1},{1,0},{2,3},{3,2},{4,5},{5,4},{6,7},{7,6},{8,9},{9,8},{10,11... | collective-permute-start | bytes 1867784 | tf_op jit(solution)/shard_map/ppermute | solution.py:58
  78.4 3.3 %collective-permute-start.19 = (bf16[128,2304]{1,0:T(8,128)(2,1)S(1)}, bf16[128,2304]{1,0:T(8,128)(2,1)S(1)}, u32[]{:S(2)}, u32[]{:S(2)}) collective-permute-start(bf16[128,2304]{1,0:T(8,128)(2,1)S(1)} %get-tuple-element.121), channel_id=1, source_target_pairs={{0,1},{1,0},{2,3},{3,2},{4,5},{5,4},{6,7},{7,6},{8,9},{9,8},{10,11... | collective-permute-start | bytes 1769480 | tf_op jit(solution)/shard_map/ppermute | solution.py:58
  82.3 17.5 %collective-permute-start.25 = (bf16[128,4736]{1,0:T(8,128)(2,1)S(1)}, bf16[128,4736]{1,0:T(8,128)(2,1)S(1)}, u32[]{:S(2)}, u32[]{:S(2)}) collective-permute-start(bf16[128,4736]{1,0:T(8,128)(2,1)S(1)} %pair_sum.4), channel_id=1, source_target_pairs={{6,0},{97,1},{0,2},{99,3},{2,4},{101,5},{4,6},{103,7},{14,8},{105,... | collective-permute-start | bytes 3637256 | tf_op jit(solution)/shard_map/ppermute | solution.py:53
  83.9 16.9 %collective-permute-start.26 = (bf16[128,4736]{1,0:T(8,128)(2,1)S(1)}, bf16[128,4736]{1,0:T(8,128)(2,1)S(1)}, u32[]{:S(2)}, u32[]{:S(2)}) collective-permute-start(bf16[128,4736]{1,0:T(8,128)(2,1)S(1)} %pair_sum.5), channel_id=1, source_target_pairs={{2,0},{33,1},{4,2},{35,3},{6,4},{37,5},{0,6},{39,7},{10,8},{41,9},... | collective-permute-start | bytes 3637256 | tf_op jit(solution)/shard_map/ppermute | solution.py:53
  91.8 3.0 %collective-permute-start.24 = (bf16[128,2432]{1,0:T(8,128)(2,1)S(1)}, bf16[128,2432]{1,0:T(8,128)(2,1)S(1)}, u32[]{:S(2)}, u32[]{:S(2)}) collective-permute-start(bf16[128,2432]{1,0:T(8,128)(2,1)S(1)} %get-tuple-element.132), channel_id=1, source_target_pairs={{0,1},{1,0},{2,3},{3,2},{4,5},{5,4},{6,7},{7,6},{8,9},{9,8},{10,11... | collective-permute-start | bytes 1867784 | tf_op jit(solution)/shard_map/ppermute | solution.py:58
  102.2 11.1 %collective-permute-start.27 = (bf16[32,5120]{1,0:T(8,128)(2,1)S(1)}, bf16[32,5120]{1,0:T(8,128)(2,1)S(1)}, u32[]{:S(2)}, u32[]{:S(2)}) collective-permute-start(bf16[32,5120]{1,0:T(8,128)(2,1)S(1)} %get-tuple-element.136), channel_id=1, source_target_pairs={{96,0},{25,1},{98,2},{27,3},{100,4},{29,5},{102,6},{31,7},{104,8},... | collective-permute-start | bytes 983048 | tf_op jit(solution)/shard_map/ppermute | solution.py:53
  105.3 8.7 %collective-permute-start.28 = (bf16[32,5120]{1,0:T(8,128)(2,1)S(1)}, bf16[32,5120]{1,0:T(8,128)(2,1)S(1)}, u32[]{:S(2)}, u32[]{:S(2)}) collective-permute-start(bf16[32,5120]{1,0:T(8,128)(2,1)S(1)} %get-tuple-element.137), channel_id=1, source_target_pairs={{64,0},{17,1},{66,2},{19,3},{68,4},{21,5},{70,6},{23,7},{72,8},{25... | collective-permute-start | bytes 983048 | tf_op jit(solution)/shard_map/ppermute | solution.py:53
  105.3 11.8 %collective-permute-start.29 = (bf16[32,5120]{1,0:T(8,128)(2,1)S(1)}, bf16[32,5120]{1,0:T(8,128)(2,1)S(1)}, u32[]{:S(2)}, u32[]{:S(2)}) collective-permute-start(bf16[32,5120]{1,0:T(8,128)(2,1)S(1)} %get-tuple-element.138), channel_id=1, source_target_pairs={{32,0},{9,1},{34,2},{11,3},{36,4},{13,5},{38,6},{15,7},{40,8},{17,... | collective-permute-start | bytes 983048 | tf_op jit(solution)/shard_map/ppermute | solution.py:53
  118.0 9.0 %collective-permute-start.30 = (f32[8,5632]{1,0:T(8,128)S(1)}, f32[8,5632]{1,0:T(8,128)S(1)}, u32[]{:S(2)}, u32[]{:S(2)}) collective-permute-start(f32[8,5632]{1,0:T(8,128)S(1)} %get-tuple-element.140), channel_id=1, source_target_pairs={{24,0},{7,1},{26,2},{1,3},{28,4},{3,5},{30,6},{5,7},{0,8},{15,9},{... | collective-permute-start | bytes 540680 | tf_op jit(solution)/shard_map/ppermute | solution.py:53
  118.3 8.6 %collective-permute-start.31 = (f32[8,5632]{1,0:T(8,128)S(1)}, f32[8,5632]{1,0:T(8,128)S(1)}, u32[]{:S(2)}, u32[]{:S(2)}) collective-permute-start(f32[8,5632]{1,0:T(8,128)S(1)} %get-tuple-element.141), channel_id=1, source_target_pairs={{16,0},{5,1},{18,2},{7,3},{20,4},{1,5},{22,6},{3,7},{24,8},{13,9},... | collective-permute-start | bytes 540680 | tf_op jit(solution)/shard_map/ppermute | solution.py:53
  120.6 7.2 %collective-permute-start.32 = (f32[8,5632]{1,0:T(8,128)S(1)}, f32[8,5632]{1,0:T(8,128)S(1)}, u32[]{:S(2)}, u32[]{:S(2)}) collective-permute-start(f32[8,5632]{1,0:T(8,128)S(1)} %get-tuple-element.142), channel_id=1, source_target_pairs={{8,0},{3,1},{10,2},{5,3},{12,4},{7,5},{14,6},{1,7},{16,8},{11,9},{... | collective-permute-start | bytes 540680 | tf_op jit(solution)/shard_map/ppermute | solution.py:53
  127.9 6.5 %collective-permute-start.34 = (f32[8,1024]{1,0:T(8,128)S(1)}, f32[8,1024]{1,0:T(8,128)S(1)}, u32[]{:S(2)}, u32[]{:S(2)}) collective-permute-start(f32[8,1024]{1,0:T(8,128)S(1)} %get-tuple-element.144.refs_0_), channel_id=1, source_target_pairs={{2,0},{33,1},{4,2},{35,3},{6,4},{37,5},{0,6},{39,7},{10,8},{41,9},... | collective-permute-start | bytes 98312 | tf_op jit(solution)/shard_map/ppermute | solution.py:53
  129.8 5.4 %collective-permute-start.35 = (f32[8,1024]{1,0:T(8,128)S(1)}, f32[8,1024]{1,0:T(8,128)S(1)}, u32[]{:S(2)}, u32[]{:S(2)}) collective-permute-start(f32[8,1024]{1,0:T(8,128)S(1)} %get-tuple-element.144.refs_0_), channel_id=1, source_target_pairs={{4,0},{65,1},{6,2},{67,3},{0,4},{69,5},{2,6},{71,7},{12,8},{73,9},... | collective-permute-start | bytes 98312 | tf_op jit(solution)/shard_map/ppermute | solution.py:53
  131.9 4.1 %collective-permute-start.36 = (f32[8,1024]{1,0:T(8,128)S(1)}, f32[8,1024]{1,0:T(8,128)S(1)}, u32[]{:S(2)}, u32[]{:S(2)}) collective-permute-start(f32[8,1024]{1,0:T(8,128)S(1)} %get-tuple-element.144.refs_0_), channel_id=1, source_target_pairs={{6,0},{97,1},{0,2},{99,3},{2,4},{101,5},{4,6},{103,7},{14,8},{105,... | collective-permute-start | bytes 98312 | tf_op jit(solution)/shard_map/ppermute | solution.py:53
  136.1 4.5 %collective-permute-start.37 = (f32[4,8,1024]{2,1,0:T(8,128)S(1)}, f32[4,8,1024]{2,1,0:T(8,128)S(1)}, u32[]{:S(2)}, u32[]{:S(2)}) collective-permute-start(f32[4,8,1024]{2,1,0:T(8,128)S(1)} %collect.3.own), channel_id=1, source_target_pairs={{0,1},{1,0},{2,3},{3,2},{4,5},{5,4},{6,7},{7,6},{8,9},{9,8},{10,11... | collective-permute-start | bytes 393224 | tf_op jit(solution)/shard_map/ppermute | solution.py:58
  136.2 11.5 %collective-permute-start.33 = (f32[8,128]{1,0:T(8,128)S(1)}, f32[8,128]{1,0:T(8,128)S(1)}, u32[]{:S(2)}, u32[]{:S(2)}) collective-permute-start(f32[8,128]{1,0:T(8,128)S(1)} %get-tuple-element.143), channel_id=1, source_target_pairs={{0,0},{1,16},{2,32},{3,17},{4,64},{5,18},{6,96},{7,19},{8,1},{9,20... | collective-permute-start | bytes 12296 | tf_op jit(solution)/shard_map/ppermute | solution.py:547
  (12 other events, 89.2 us)
